TPU v7x, 512 devices: a whole 4x4x16 slice. The times are simulated.
512 devices in a mesh: group: 16 (over y, x), dev: 32 (over z, core).
Axes of the slice: x: 4, y: 4, z: 16, core: 2. Of those that a mesh axis runs over, the one named last changes fastest.
Arguments:
- cam_jac: float32 [18, 2162688], P(None, ('group', 'dev')), may hold values from -1 to 1
- point_jac: float32 [6, 2162688], P(None, ('group', 'dev')), may hold values from -3 to 3
- residuals: float32 [2, 2162688], P(None, ('group', 'dev')), may hold values from -15 to 15
- obs_camera: int32 [2162688], P(('group', 'dev')), may hold values from 0 to 127
- obs_point: int32 [2162688], P(('group', 'dev')), may hold values from 0 to 1023
- obs_count: int32 [512, 33], P(('group', 'dev')), may hold values from 42 to 128, as said below
- cam_damp: float32 [9, 65536], P(None, ('group', 'dev')), may hold values from 0.3 to 3
- pt_damp: float32 [3, 524288], P(None, ('group', 'dev')), may hold values from 0.3 to 3
- partner_mask: int32 [32], P('dev'), may hold values from 1 to 15
Outputs:
- update: float32 [9, 65536], P(None, ('group', 'dev'))
- remainder: float32 [9, 65536], P(None, ('group', 'dev'))
Inputs may be any that keep to these rules, and one draw needn't show every extreme that they name: `obs_count`: slots at or beyond a count are padding. Every device's row holds one count equal to 128. For each index d within a partition, partitions g and g XOR partner_mask[d] are matched.
All inputs are finite; a program needn't handle non-finite values.
Results may differ from a plain program's by a relative error of at most 0.0085.
Values sent between devices are 32-bit elements; how exact they have to be, the bound alone decides.
No kernel may reach another device: no remote copies, remote signals or barrier semaphores. Data moves between devices by JAX's collectives and lax.ppermute only.
A program may use at most 64 MiB of HBM per device.

v0:
```python
import jax
import jax.numpy as jnp
from jax import lax
from jax.sharding import PartitionSpec as P

ITERS = 2


def partner_2(block, axis, distance):
    count = lax.axis_size(axis)
    route = []
    for low in range(count):
        high = low | 1 << distance
        if high != low and high < count:
            route += [(low, high), (high, low)]
    return lax.ppermute(block, axis, route)


def seg_rows(entries, indices, item_count):
    return jax.vmap(lambda single: jax.ops.segment_sum(single, indices, num_segments=item_count))(
        entries
    )


def cam_apply(cam_rows, cam_values):
    first_row = jnp.sum(cam_rows[0:9] * cam_values, axis=0)
    second_row = jnp.sum(cam_rows[9:18] * cam_values, axis=0)
    return jnp.stack([first_row, second_row])


def cam_spread(cam_rows, slot_values):
    return cam_rows[0:9] * slot_values[0:1] + cam_rows[9:18] * slot_values[1:2]


def point_apply(point_rows, point_values):
    first_row = jnp.sum(point_rows[0:3] * point_values, axis=0)
    second_row = jnp.sum(point_rows[3:6] * point_values, axis=0)
    return jnp.stack([first_row, second_row])


def point_spread(point_rows, slot_values):
    return point_rows[0:3] * slot_values[0:1] + point_rows[3:6] * slot_values[1:2]


def point_blocks(point_rows, point_ids, damping):
    item_count = damping.shape[1]
    summands = []
    for first_axis, second_axis in ((0, 0), (0, 1), (0, 2), (1, 1), (1, 2), (2, 2)):
        summands.append(
            point_rows[first_axis] * point_rows[second_axis]
            + point_rows[3 + first_axis] * point_rows[3 + second_axis]
        )
    blocks = seg_rows(jnp.stack(summands), point_ids, item_count)
    nothing = jnp.zeros_like(damping[0])
    return blocks + jnp.stack([damping[0], nothing, nothing, damping[1], nothing, damping[2]])


def solve_three(blocks, source):
    cofactor_xx = blocks[3] * blocks[5] - blocks[4] * blocks[4]
    cofactor_xy = blocks[2] * blocks[4] - blocks[1] * blocks[5]
    cofactor_xz = blocks[1] * blocks[4] - blocks[2] * blocks[3]
    cofactor_yy = blocks[0] * blocks[5] - blocks[2] * blocks[2]
    cofactor_yz = blocks[1] * blocks[2] - blocks[0] * blocks[4]
    cofactor_zz = blocks[0] * blocks[3] - blocks[1] * blocks[1]
    determinant = blocks[0] * cofactor_xx + blocks[1] * cofactor_xy + blocks[2] * cofactor_xz
    first_out = cofactor_xx * source[0] + cofactor_xy * source[1] + cofactor_xz * source[2]
    second_out = cofactor_xy * source[0] + cofactor_yy * source[1] + cofactor_yz * source[2]
    third_out = cofactor_xz * source[0] + cofactor_yz * source[1] + cofactor_zz * source[2]
    return jnp.stack([first_out, second_out, third_out]) / determinant


def across(values, partner, swapper, bit_count):
    for bit_index in range(bit_count):
        moved = swapper(values, bit_index)
        chosen = jnp.bitwise_and(jnp.right_shift(partner, bit_index), 1) == 1
        values = jnp.where(chosen, moved, values)
    return values


def on_device(
    cam_jac, point_jac, residuals, obs_camera, obs_point, obs_count, cam_damp, pt_damp, partner_mask
):
    members = lax.axis_size("dev")
    bit_count = lax.axis_size("group").bit_length() - 1
    block_count = members + 1
    slot_total = cam_jac.shape[1]
    slot_size = slot_total // block_count
    inner_total = members * slot_size
    cam_count = cam_damp.shape[1]
    point_count = pt_damp.shape[1]
    partner = partner_mask[0]
    live = (
        (jnp.arange(slot_size, dtype=jnp.int32)[None, :] < obs_count[0][:, None])
        .reshape(-1)
        .astype(jnp.float32)
    )
    cam_rows = cam_jac * live
    point_rows = point_jac * live
    blocks = point_blocks(point_rows, obs_point, pt_damp)

    def point_side(moved):
        pulled = solve_three(
            blocks, seg_rows(point_spread(point_rows, moved), obs_point, point_count)
        )
        return moved - point_apply(point_rows, pulled[:, obs_point])

    reduced = point_side(residuals)
    payload = jnp.concatenate([cam_rows, reduced, obs_camera.astype(jnp.float32)[None, :]], 0)
    arrived_inner = lax.all_to_all(
        payload[:, :inner_total], "dev", split_axis=1, concat_axis=1, tiled=True
    )
    arrived_outer = across(
        payload[:, inner_total:],
        partner,
        lambda values, bit_index: partner_2(values, "group", bit_index),
        bit_count,
    )
    arrived = jnp.concatenate([arrived_inner, arrived_outer], 1)
    owned_rows = arrived[0:18]
    owned_ids = arrived[20].astype(jnp.int32)
    gradient = -seg_rows(cam_spread(owned_rows, arrived[18:20]), owned_ids, cam_count)
    diagonal = cam_damp + seg_rows(
        owned_rows[0:9] ** 2 + owned_rows[9:18] ** 2, owned_ids, cam_count
    )

    def schur(direction):
        moved = cam_apply(owned_rows, direction[:, owned_ids])
        sent_inner = lax.all_to_all(
            moved[:, :inner_total], "dev", split_axis=1, concat_axis=1, tiled=True
        )
        sent_outer = across(
            moved[:, inner_total:],
            partner,
            lambda values, bit_index: partner_2(values, "group", bit_index),
            bit_count,
        )
        kept = point_side(jnp.concatenate([sent_inner, sent_outer], 1))
        back_inner = lax.all_to_all(
            kept[:, :inner_total], "dev", split_axis=1, concat_axis=1, tiled=True
        )
        back_outer = across(
            kept[:, inner_total:],
            partner,
            lambda values, bit_index: partner_2(values, "group", bit_index),
            bit_count,
        )
        returned = jnp.concatenate([back_inner, back_outer], 1)
        return cam_damp * direction + seg_rows(
            cam_spread(owned_rows, returned), owned_ids, cam_count
        )

    precond = 1.0 / diagonal
    update = jnp.zeros_like(gradient)
    remainder = gradient
    scaled = precond * remainder
    direction = scaled
    norm_now = lax.psum(jnp.sum(remainder * scaled), ("group", "dev"))
    for step_index in range(ITERS):
        image = schur(direction)
        curvature = lax.psum(jnp.sum(direction * image), ("group", "dev"))
        step_size = norm_now / curvature
        update = update + step_size * direction
        remainder = remainder - step_size * image
        if step_index + 1 < ITERS:
            scaled = precond * remainder
            norm_next = lax.psum(jnp.sum(remainder * scaled), ("group", "dev"))
            direction = scaled + norm_next / norm_now * direction
            norm_now = norm_next
    return (update, remainder)


def solution(mesh):
    return jax.shard_map(
        on_device,
        mesh=mesh,
        in_specs=(
            P(None, ("group", "dev")),
            P(None, ("group", "dev")),
            P(None, ("group", "dev")),
            P(("group", "dev")),
            P(("group", "dev")),
            P(("group", "dev"), None),
            P(None, ("group", "dev")),
            P(None, ("group", "dev")),
            P("dev"),
        ),
        out_specs=(P(None, ("group", "dev")), P(None, ("group", "dev"))),
        check_vma=False,
    )
```

profile of v0, /device:TPU:1, one launch (start us, length us, event | category | flops | bytes accessed | tf_op | source)
XLA Modules:
  0.0 864.4 jit_solution(16352821904402981239)
XLA Ops:
  1.4 2.9 copy.240
  4.3 3.0 broadcast_multiply_fusion
  7.3 7.5 fusion.96
  31.1 25.9 %scatter_fusion = f32[6,1024]{0,1:T(8,128)S(1)} fusion(f32[6,1024]{0,1:T(8,128)S(1)} %copy.265, s32[4224]{0:T(1024)S(1)} %copy-done.11, f32[4224,6]{1,0:T(8,128)} %copy.266), kind=kCustom, calls=%fused_computation.5 | custom fusion | flops 25344 | bytes 321024 | tf_op jit(solution)/shard_map/vmap()/scatter-add | solution.py:20
  64.6 28.7 %scatter_custom_fusion.1 = f32[3,1024]{0,1:T(8,128)S(1)} fusion(s32[4224]{0:T(1024)S(1)} %copy-done.11, f32[6,4224]{0,1:T(8,128)S(1)} %broadcast_multiply_fusion, f32[4224]{0:T(1024)S(1)} %get-tuple-element.37, f32[4224]{0:T(1024)S(1)} %get-tuple-element.36, f32[]{:T(128)} %constant.12.clone.1), kind=kCustom, calls=%fused_computation.45 | custom fusion | flops 50688 | bytes 4378628 | tf_op jit(solution)/shard_map/vmap()/scatter-add | solution.py:20
  98.9 8.7 %gather_fusion = f32[4224,3]{1,0:T(8,128)} fusion(f32[3,1024]{0,1:T(8,128)S(1)} %copy.276, s32[5120]{0:T(1024)S(1)} %pad_clamp_fusion.1), kind=kCustom, calls=%fused_computation | custom fusion | bytes 118272 | tf_op jit(solution)/shard_map/gather | solution.py:105
  107.6 3.4 fusion.21
  112.4 16.7 %all-to-all-start = ((f32[21,32,128]{2,0,1:T(8,128)}), f32[21,32,128]{2,0,1:T(8,128)S(1)}, u32[]{:S(2)}, u32[]{:S(2)}) async-start(f32[21,32,128]{2,0,1:T(8,128)} %copy.277), calls=%async_computation | async-start | bytes 786432 | tf_op jit(solution)/shard_map/all_to_all | solution.py:109
  129.1 3.1 collective-permute-start
  133.6 4.6 collective-permute-start.1
  139.8 3.2 collective-permute-start.2
  144.5 4.8 collective-permute-start.3
  150.5 6.6 all-to-all-done
  161.9 26.1 %scatter_custom_fusion.3 = f32[9,128]{0,1:T(8,128)S(1)} fusion(f32[9,128]{0,1:T(8,128)S(1)} %copy.314, s32[4224]{0:T(1024)S(1)} %reduce.2, f32[9,4224]{0,1:T(8,128)} %copy.304, f32[9,4224]{0,1:T(8,128)} %copy.303), kind=kCustom, calls=%fused_computation.37 | custom fusion | flops 152064 | bytes 308736 | tf_op jit(solution)/shard_map/vmap()/scatter-add | solution.py:20
  188.0 28.5 %scatter_custom_fusion.2 = f32[9,128]{0,1:T(8,128)S(1)} fusion(s32[4224]{0:T(1024)S(1)} %reduce.2, f32[9,4224]{0,1:T(8,128)} %copy.304, f32[9,4224]{0,1:T(8,128)} %copy.303, f32[4224]{0:T(1024)S(1)} %get-tuple-element.25, f32[4224]{0:T(1024)S(1)} %get-tuple-element.24, f32[]{:T(128)} %constant.12.clone.1), kind=kCustom, calls=%fused_computation.39 | custom fusion | flops 152064 | bytes 349700 | tf_op jit(solution)/shard_map/vmap()/scatter-add | solution.py:20
  216.6 8.7 %gather_fusion.1 = f32[4224,9]{1,0:T(8,128)} fusion(f32[9,128]{0,1:T(8,128)S(1)} %get-tuple-element.47, s32[5120]{0:T(1024)S(1)} %pad_clamp_fusion), kind=kCustom, calls=%fused_computation.1 | custom fusion | bytes 321024 | tf_op jit(solution)/shard_map/gather | solution.py:127
  225.3 4.1 fusion.15
  229.5 3.1 collective-permute-start.4
  233.8 4.7 collective-permute-start.5
  239.6 3.2 collective-permute-start.6
  243.9 4.8 collective-permute-start.7
  249.4 13.3 %all-to-all-start.1 = ((f32[2,32,128]{2,0,1:T(2,128)}), f32[2,32,128]{2,0,1:T(2,128)S(1)}, u32[]{:S(2)}, u32[]{:S(2)}) async-start(f32[2,32,128]{2,0,1:T(2,128)} %fusion.73), calls=%async_computation.1 | async-start | bytes 65536 | tf_op jit(solution)/shard_map/all_to_all | solution.py:128
  262.7 12.1 %all-to-all-done.1 = f32[2,32,128]{2,0,1:T(2,128)S(1)} async-done(((f32[2,32,128]{2,0,1:T(2,128)}), f32[2,32,128]{2,0,1:T(2,128)S(1)}, u32[]{:S(2)}, u32[]{:S(2)}) %all-to-all-start.1) | async-done | bytes 32800 | tf_op jit(solution)/shard_map/all_to_all | solution.py:128
  275.4 28.8 %scatter_custom_fusion.4 = f32[3,1024]{0,1:T(8,128)S(1)} fusion(s32[4224]{0:T(1024)} %param.13, f32[6,4224]{0,1:T(8,128)S(1)} %broadcast_multiply_fusion, f32[4224]{0:T(1024)S(1)} %get-tuple-element.35, f32[4224]{0:T(1024)S(1)} %get-tuple-element.34, f32[]{:T(128)} %constant.12.clone.1), kind=kCustom, calls=%fused_computation.31 | custom fusion | flops 50688 | bytes 4379136 | tf_op jit(solution)/shard_map/vmap()/scatter-add | solution.py:20
  309.8 9.5 %gather_fusion.2 = f32[4224,3]{1,0:T(8,128)} fusion(f32[3,1024]{0,1:T(8,128)S(1)} %copy.286, s32[5120]{0:T(1024)} %copy-done.4), kind=kCustom, calls=%fused_computation.2 | custom fusion | bytes 118272 | tf_op jit(solution)/shard_map/gather | solution.py:105
  319.3 3.4 fusion.11
  322.8 3.1 collective-permute-start.8
  327.1 4.6 collective-permute-start.9
  340.3 8.0 all-to-all-start.2
  348.3 12.3 %all-to-all-done.2 = f32[2,32,128]{2,0,1:T(2,128)S(1)} async-done(((f32[2,32,128]{2,0,1:T(2,128)}), f32[2,32,128]{2,0,1:T(2,128)S(1)}, u32[]{:S(2)}, u32[]{:S(2)}) %all-to-all-start.2) | async-done | bytes 32800 | tf_op jit(solution)/shard_map/all_to_all | solution.py:138
  360.7 29.0 %scatter_custom_fusion.5 = f32[9,128]{0,1:T(8,128)S(1)} fusion(f32[9,128]{0,1:T(8,128)S(1)} %get-tuple-element.46, s32[4224]{0:T(1024)} %copy-done.17, f32[9,4224]{0,1:T(8,128)} %copy.304, f32[9,4224]{0,1:T(8,128)} %copy.303, f32[4224]{0:T(1024)S(1)} %get-tuple-element.33, f32[4224]{0:T(1024)S(1)} %get-tuple-element.32), kind=kCustom, calls=%fused_computation.25 | custom fusion | flops 152064 | bytes 4370944 | tf_op jit(solution)/shard_map/vmap()/scatter-add | solution.py:20
  390.3 101.9 %all-reduce = (f32[]{:T(128)}, f32[]{:T(128)}) all-reduce(f32[]{:T(128)} %get-tuple-element.27, f32[]{:T(128)} %get-tuple-element.26), channel_id=1, replica_groups=mesh['group'=16,'dev'=32] {'group','dev'}, use_global_device_ids=true, to_apply=%region_7.8 | all-reduce | flops 2 | bytes 16 | tf_op jit(solution)/shard_map/psum | solution.py:157
  494.1 99.5 %psum.30 = f32[]{:T(128)} all-reduce(f32[]{:T(128)} %get-tuple-element.42), channel_id=1, replica_groups=mesh['group'=16,'dev'=32] {'group','dev'}, use_global_device_ids=true, to_apply=%region_17.18 | all-reduce | flops 1 | bytes 8 | tf_op jit(solution)/shard_map/psum | solution.py:166
  595.0 8.7 %gather_fusion.3 = f32[4224,9]{1,0:T(8,128)} fusion(f32[9,128]{0,1:T(8,128)S(1)} %get-tuple-element.41, s32[5120]{0:T(1024)S(1)} %copy-done.9), kind=kCustom, calls=%fused_computation.3 | custom fusion | bytes 321024 | tf_op jit(solution)/shard_map/gather | solution.py:127
  603.7 4.1 fusion.7
  612.2 3.1 collective-permute-start.13
  622.4 3.2 collective-permute-start.15
  626.2 10.0 %all-to-all-start.3 = ((f32[2,32,128]{2,0,1:T(2,128)}), f32[2,32,128]{2,0,1:T(2,128)S(1)}, u32[]{:S(2)}, u32[]{:S(2)}) async-start(f32[2,32,128]{2,0,1:T(2,128)} %fusion.71), calls=%async_computation.3 | async-start | bytes 65536 | tf_op jit(solution)/shard_map/all_to_all | solution.py:128
  636.2 12.1 %all-to-all-done.3 = f32[2,32,128]{2,0,1:T(2,128)S(1)} async-done(((f32[2,32,128]{2,0,1:T(2,128)}), f32[2,32,128]{2,0,1:T(2,128)S(1)}, u32[]{:S(2)}, u32[]{:S(2)}) %all-to-all-start.3) | async-done | bytes 32800 | tf_op jit(solution)/shard_map/all_to_all | solution.py:128
  648.4 29.0 %scatter_custom_fusion.6 = f32[3,1024]{0,1:T(8,128)S(1)} fusion(s32[4224]{0:T(1024)} %param.13, f32[6,4224]{0,1:T(8,128)S(1)} %broadcast_multiply_fusion, f32[4224]{0:T(1024)S(1)} %get-tuple-element.31, f32[4224]{0:T(1024)S(1)} %get-tuple-element.30, f32[]{:T(128)} %constant.12.clone.1), kind=kCustom, calls=%fused_computation.19 | custom fusion | flops 50688 | bytes 4379136 | tf_op jit(solution)/shard_map/vmap()/scatter-add | solution.py:20
  681.7 8.7 %gather_fusion.4 = f32[4224,3]{1,0:T(8,128)} fusion(f32[3,1024]{0,1:T(8,128)S(1)} %copy.291, s32[5120]{0:T(1024)S(1)} %copy-done.5), kind=kCustom, calls=%fused_computation.4 | custom fusion | bytes 118272 | tf_op jit(solution)/shard_map/gather | solution.py:105
  690.4 3.4 fusion.3
  701.0 3.1 collective-permute-done.17
  708.4 3.6 collective-permute-start.19
  712.5 8.3 all-to-all-start.4
  720.9 12.3 %all-to-all-done.4 = f32[2,32,128]{2,0,1:T(2,128)S(1)} async-done(((f32[2,32,128]{2,0,1:T(2,128)}), f32[2,32,128]{2,0,1:T(2,128)S(1)}, u32[]{:S(2)}, u32[]{:S(2)}) %all-to-all-start.4) | async-done | bytes 32800 | tf_op jit(solution)/shard_map/all_to_all | solution.py:138
  733.2 28.6 %scatter_custom_fusion.7 = f32[9,128]{0,1:T(8,128)S(1)} fusion(f32[9,128]{0,1:T(8,128)S(1)} %get-tuple-element.40, s32[4224]{0:T(1024)} %copy-done.17, f32[9,4224]{0,1:T(8,128)} %copy.304, f32[9,4224]{0,1:T(8,128)} %copy.303, f32[4224]{0:T(1024)S(1)} %get-tuple-element.29, f32[4224]{0:T(1024)S(1)} %get-tuple-element.28), kind=kCustom, calls=%fused_computation.13 | custom fusion | flops 152064 | bytes 4370944 | tf_op jit(solution)/shard_map/vmap()/scatter-add | solution.py:20
  762.5 99.0 %psum.31 = f32[]{:T(128)} all-reduce(f32[]{:T(128)} %multiply_reduce_fusion), channel_id=1, replica_groups=mesh['group'=16,'dev'=32] {'group','dev'}, use_global_device_ids=true, to_apply=%region_25.26 | all-reduce | flops 1 | bytes 8 | tf_op jit(solution)/shard_map/psum | solution.py:160
  (192 shorter events, 92.8 us)
Async XLA Ops:
  26.1 4.6 copy-start.20
  28.4 2.7 copy-start.11
  59.1 5.0 copy-start
  59.1 5.4 copy-start.10
  97.3 1.3 copy-start.12
  98.8 12.2 %copy-start.4 = (s32[5120]{0:T(1024)}, s32[5120]{0:T(1024)S(1)}, u32[]{:S(2)}) copy-start(s32[5120]{0:T(1024)S(1)} %pad_clamp_fusion.1) | copy-start | bytes 61444
  107.6 3.5 copy-start.3
  107.6 3.5 copy-start.16
  111.3 38.1 %copy-start.21 = (f32[9,128]{1,0:T(8,128)S(1)}, f32[9,128]{1,0:T(8,128)}, u32[]{:S(2)}) copy-start(f32[9,128]{1,0:T(8,128)} %param.15) | copy-start | bytes 13828
  112.4 44.7 %all-to-all-start = ((f32[21,32,128]{2,0,1:T(8,128)}), f32[21,32,128]{2,0,1:T(8,128)S(1)}, u32[]{:S(2)}, u32[]{:S(2)}) async-start(f32[21,32,128]{2,0,1:T(8,128)} %copy.277), calls=%async_computation | async-start | bytes 786432 | tf_op jit(solution)/shard_map/all_to_all | solution.py:109
  129.1 4.4 collective-permute-start
  133.6 6.2 collective-permute-start.1
  139.8 4.7 collective-permute-start.2
  144.5 5.9 collective-permute-start.3
  161.8 54.8 %copy-start.8 = (s32[5120]{0:T(1024)}, s32[5120]{0:T(1024)S(1)}, u32[]{:S(2)}) copy-start(s32[5120]{0:T(1024)S(1)} %pad_clamp_fusion) | copy-start | bytes 61444
  161.8 26.1 %copy-start.17 = (s32[4224]{0:T(1024)}, s32[4224]{0:T(1024)S(1)}, u32[]{:S(2)}) copy-start(s32[4224]{0:T(1024)S(1)} %reduce.2) | copy-start | bytes 50692
  229.5 4.3 collective-permute-start.4
  233.8 5.8 collective-permute-start.5
  239.6 4.3 collective-permute-start.6
  243.9 18.8 %collective-permute-start.7 = (f32[2,128]{1,0:T(2,128)S(1)}, f32[2,128]{1,0:T(2,128)S(1)}, u32[]{:S(2)}, u32[]{:S(2)}) collective-permute-start(f32[2,128]{1,0:T(2,128)S(1)} %broadcast_select_fusion.15), channel_id=1, source_target_pairs={{0,256},{256,0},{32,288},{288,32},{64,320},{320,64},{96,352},{352,... | collective-permute-start | bytes 3080 | tf_op jit(solution)/shard_map/ppermute | solution.py:16
  249.4 25.4 %all-to-all-start.1 = ((f32[2,32,128]{2,0,1:T(2,128)}), f32[2,32,128]{2,0,1:T(2,128)S(1)}, u32[]{:S(2)}, u32[]{:S(2)}) async-start(f32[2,32,128]{2,0,1:T(2,128)} %fusion.73), calls=%async_computation.1 | async-start | bytes 65536 | tf_op jit(solution)/shard_map/all_to_all | solution.py:128
  262.7 12.7 %copy-start.18 = (f32[2,128]{1,0:T(2,128)}, f32[2,128]{1,0:T(2,128)S(1)}, u32[]{:S(2)}) copy-start(f32[2,128]{1,0:T(2,128)S(1)} %broadcast_select_fusion.19) | copy-start | bytes 3076
  274.8 0.6 copy-start.6
  319.3 3.4 copy-start.7
  319.3 3.4 copy-start.19
  322.8 4.3 collective-permute-start.8
  327.1 5.8 collective-permute-start.9
  332.9 4.3 collective-permute-start.10
  337.2 11.1 %collective-permute-start.11 = (f32[2,128]{1,0:T(2,128)S(1)}, f32[2,128]{1,0:T(2,128)S(1)}, u32[]{:S(2)}, u32[]{:S(2)}) collective-permute-start(f32[2,128]{1,0:T(2,128)S(1)} %broadcast_select_fusion.14), channel_id=1, source_target_pairs={{0,256},{256,0},{32,288},{288,32},{64,320},{320,64},{96,352},{352,... | collective-permute-start | bytes 3080 | tf_op jit(solution)/shard_map/ppermute | solution.py:16
  340.3 20.3 %all-to-all-start.2 = ((f32[2,32,128]{2,0,1:T(2,128)}), f32[2,32,128]{2,0,1:T(2,128)S(1)}, u32[]{:S(2)}, u32[]{:S(2)}) async-start(f32[2,32,128]{2,0,1:T(2,128)} %slice_bitcast_fusion.1), calls=%async_computation.2 | async-start | bytes 65536 | tf_op jit(solution)/shard_map/all_to_all | solution.py:138
  360.7 234.3 %copy-start.9 = (s32[5120]{0:T(1024)S(1)}, s32[5120]{0:T(1024)}, u32[]{:S(2)}) copy-start(s32[5120]{0:T(1024)} %copy-done.8) | copy-start | bytes 61444
  494.1 113.7 %copy-start.1 = (f32[9,128]{0,1:T(8,128)}, f32[9,128]{0,1:T(8,128)S(1)}, u32[]{:S(2)}) copy-start(f32[9,128]{0,1:T(8,128)S(1)} %get-tuple-element.43) | copy-start | bytes 13828
  607.9 4.3 collective-permute-start.12
  612.2 5.8 collective-permute-start.13
  618.1 4.3 collective-permute-start.14
  622.4 13.8 %collective-permute-start.15 = (f32[2,128]{1,0:T(2,128)S(1)}, f32[2,128]{1,0:T(2,128)S(1)}, u32[]{:S(2)}, u32[]{:S(2)}) collective-permute-start(f32[2,128]{1,0:T(2,128)S(1)} %broadcast_select_fusion.13), channel_id=1, source_target_pairs={{0,256},{256,0},{32,288},{288,32},{64,320},{320,64},{96,352},{352,... | collective-permute-start | bytes 3080 | tf_op jit(solution)/shard_map/ppermute | solution.py:16
  626.2 22.1 %all-to-all-start.3 = ((f32[2,32,128]{2,0,1:T(2,128)}), f32[2,32,128]{2,0,1:T(2,128)S(1)}, u32[]{:S(2)}, u32[]{:S(2)}) async-start(f32[2,32,128]{2,0,1:T(2,128)} %fusion.71), calls=%async_computation.3 | async-start | bytes 65536 | tf_op jit(solution)/shard_map/all_to_all | solution.py:128
  677.4 3.9 copy-start.14
  677.5 3.9 copy-start.15
  677.5 4.0 copy-start.13
  677.5 4.2 copy-start.5
  693.9 4.3 collective-permute-start.16
  698.2 5.8 collective-permute-start.17
  704.1 4.3 collective-permute-start.18
  708.4 12.5 %collective-permute-start.19 = (f32[2,128]{1,0:T(2,128)S(1)}, f32[2,128]{1,0:T(2,128)S(1)}, u32[]{:S(2)}, u32[]{:S(2)}) collective-permute-start(f32[2,128]{1,0:T(2,128)S(1)} %broadcast_select_fusion.12), channel_id=1, source_target_pairs={{0,256},{256,0},{32,288},{288,32},{64,320},{320,64},{96,352},{352,... | collective-permute-start | bytes 3080 | tf_op jit(solution)/shard_map/ppermute | solution.py:16
  712.5 20.6 %all-to-all-start.4 = ((f32[2,32,128]{2,0,1:T(2,128)}), f32[2,32,128]{2,0,1:T(2,128)S(1)}, u32[]{:S(2)}, u32[]{:S(2)}) async-start(f32[2,32,128]{2,0,1:T(2,128)} %slice_bitcast_fusion), calls=%async_computation.4 | async-start | bytes 65536 | tf_op jit(solution)/shard_map/all_to_all | solution.py:138
  733.2 129.6 %copy-start.2 = (f32[9,128]{0,1:T(8,128)S(1)}, f32[9,128]{0,1:T(8,128)}, u32[]{:S(2)}) copy-start(f32[9,128]{0,1:T(8,128)} %copy-done.1) | copy-start | bytes 13828
where the time goes:
time: 873 us; the launch traced here: 864 us
  blocking collectives  300 us (34%)
  other arithmetic  254 us (29%)
  starting transfers between devices  122 us (14%)
  local copies, waits for them, and re-layouts  99.9 us (11%)
  waiting for transfers between devices  81.4 us (9%)
    scatter-add x8, other arithmetic, seg_rows(): jax.ops.segment_sum(single, indices, num_segments=item_count)  225 us
    psum x1, blocking collectives, on_device(): norm_now = lax.psum(jnp.sum(remainder * scaled), ('group', 'dev'))  102 us
    psum x1, blocking collectives, on_device(): norm_next = lax.psum(jnp.sum(remainder * scaled), ('group', 'dev'))  99.5 us
    psum x1, blocking collectives, on_device(): curvature = lax.psum(jnp.sum(direction * image), ('group', 'dev'))  99 us
    ppermute x20, starting transfers between devices, partner_2(): return lax.ppermute(block, axis, route)  66 us
    gather x3, local copies, waits for them, and re-layouts, point_side(): return moved - point_apply(point_rows, pulled[:, obs_point])  26.9 us
    ppermute x20, waiting for transfers between devices, partner_2(): return lax.ppermute(block, axis, route)  26.1 us
    all_to_all x2, waiting for transfers between devices, schur(): lax.all_to_all(kept[:, :inner_total], 'dev', split_axis=1, concat_axis=1,...  24.5 us
  transfers between devices with their start and end apart: 25, of which 21 were waited for; matrix products, arithmetic and copies ran while one was open for 0% of the time, Pallas kernels for 0%

commit v1 on v0

v1 whole, which is shorter than its diff:
```python
import jax
import jax.numpy as jnp
from jax import lax
from jax.experimental import pallas as pl
from jax.experimental.pallas import tpu as pltpu
from jax.sharding import PartitionSpec as P

F32 = jnp.float32
BF16 = jnp.bfloat16
PAIRS = ((0, 0), (0, 1), (0, 2), (1, 1), (1, 2), (2, 2))


def one_hot(ids, count):
    rows = lax.broadcasted_iota(jnp.int32, (count, ids.shape[1]), 0)
    return jnp.where(rows == ids, 1.0, 0.0).astype(BF16)


def pieces(values, count):
    found = []
    for _ in range(count - 1):
        found.append(values.astype(BF16).astype(F32))
        values = values - found[-1]
    return found + [values]


def collect(values, chosen, count=2):
    m = values.shape[0]
    stacked = jnp.concatenate(pieces(values, count), 0).astype(BF16)
    sums = lax.dot_general(
        stacked, chosen, (((1,), (1,)), ((), ())), preferred_element_type=F32
    )
    total = sums[0:m]
    for i in range(1, count):
        total = total + sums[i * m : (i + 1) * m]
    return total


def fetch(items, chosen):
    stacked = jnp.concatenate(pieces(items, 2), 1).astype(BF16)
    return jnp.dot(
        stacked, jnp.concatenate([chosen, chosen], 0), preferred_element_type=F32
    )


def col_sum(values):
    return jnp.sum(values, axis=0, keepdims=True)


def total(values):
    return jnp.sum(values, keepdims=True)


def lane_blocks(row):
    out = row[:, 0:128]
    for b in range(1, row.shape[1] // 128):
        out = out + row[:, b * 128 : (b + 1) * 128]
    return out


def put_payload(in_ref, out_ref, first, second, extra):
    inner = in_ref.shape[1]
    in_ref[0:1, :] = first[:, :inner]
    in_ref[1:2, :] = second[:, :inner]
    in_ref[2:3, :] = jnp.concatenate([extra] * (inner // 128), 1)
    out_ref[0:1, :] = first[:, inner:]
    out_ref[1:2, :] = second[:, inner:]


def row_of(in_ref, group_ref, partner, r):
    return jnp.concatenate([in_ref[r : r + 1, :], group_ref[partner, r : r + 1, :]], 1)


def group_total(group_ref):
    row = jnp.zeros((1, 128), F32)
    for i in range(group_ref.shape[0]):
        row = row + group_ref[i, 2:3, :]
    return total(row)


def solve_points(inverse, sums):
    c = [inverse[8 * i : 8 * i + 8] for i in range(6)]
    g = [sums[8 * i : 8 * i + 8] for i in range(3)]
    return jnp.concatenate(
        [
            c[0] * g[0] + c[1] * g[1] + c[2] * g[2],
            c[1] * g[0] + c[3] * g[1] + c[4] * g[2],
            c[2] * g[0] + c[4] * g[1] + c[5] * g[2],
        ],
        0,
    )


def spread_points(placed, first, second):
    return jnp.concatenate(
        [
            placed[8 * r : 8 * r + 8] * first + placed[24 + 8 * r : 32 + 8 * r] * second
            for r in range(3)
        ],
        0,
    )


def pull_points(placed, pulled, first, second):
    v0 = placed[0:8] * pulled[0:8] + placed[8:16] * pulled[8:16] + placed[16:24] * pulled[16:24]
    v1 = placed[24:32] * pulled[0:8] + placed[32:40] * pulled[8:16] + placed[40:48] * pulled[16:24]
    return first - col_sum(v0), second - col_sum(v1)


def setup_kernel(
    count_ref, cam_ref, point_ref, res_ref, cam_id_ref, point_id_ref, damp_ref,
    in_ref, group_ref, placed_ref, inverse_ref,
):
    n = cam_ref.shape[1]
    inner = n - 128
    lanes = lax.broadcasted_iota(jnp.int32, (1, 128), 1)
    live = jnp.concatenate(
        [jnp.where(lanes < count_ref[0, b], 1.0, 0.0) for b in range(n // 128)], 1
    )
    ids = point_id_ref[...]
    chosen = one_hot(jnp.bitwise_and(ids, 127), 128)
    high = jnp.right_shift(ids, 7)
    digit = jnp.where(lax.broadcasted_iota(jnp.int32, (8, n), 0) == high, live, 0.0)
    for r in range(6):
        placed_ref[8 * r : 8 * r + 8, :] = digit * point_ref[r : r + 1, :]
    placed = placed_ref[...]
    part = [placed[8 * r : 8 * r + 8] for r in range(6)]
    first, second = res_ref[0:1, :], res_ref[1:2, :]
    squares = [part[a] * part[b] + part[3 + a] * part[3 + b] for a, b in PAIRS]
    blocks = collect(jnp.concatenate(squares, 0), chosen, 3)
    sums = collect(spread_points(placed, first, second), chosen)
    b = [blocks[8 * i : 8 * i + 8] for i in range(6)]
    for axis, entry in ((0, 0), (1, 3), (2, 5)):
        damp = damp_ref[axis : axis + 1, :]
        b[entry] = b[entry] + jnp.concatenate(
            [damp[:, 128 * h : 128 * h + 128] for h in range(8)], 0
        )
    cof = [
        b[3] * b[5] - b[4] * b[4],
        b[2] * b[4] - b[1] * b[5],
        b[1] * b[4] - b[2] * b[3],
        b[0] * b[5] - b[2] * b[2],
        b[1] * b[2] - b[0] * b[4],
        b[0] * b[3] - b[1] * b[1],
    ]
    det = b[0] * cof[0] + b[1] * cof[1] + b[2] * cof[2]
    inverse = jnp.concatenate([c / det for c in cof], 0)
    inverse_ref[...] = inverse
    pulled = fetch(solve_points(inverse, sums), chosen)
    first, second = pull_points(placed, pulled, first, second)
    rows = cam_ref[...] * live
    cam_ids = cam_id_ref[...].astype(F32)

    def put(ref, i, lo):
        hi = lo + 128
        ref[i, 0:18, :] = rows[:, lo:hi]
        ref[i, 18:19, :] = first[:, lo:hi]
        ref[i, 19:20, :] = second[:, lo:hi]
        ref[i, 20:21, :] = cam_ids[:, lo:hi]
        ref[i, 21:24, :] = jnp.zeros((3, 128), F32)

    for i in range(in_ref.shape[0]):
        put(in_ref, i, 128 * i)
    for i in range(group_ref.shape[0]):
        put(group_ref, i, inner)


def cam_rows_of(in_ref, group_ref, partner):
    blocks = [in_ref[i] for i in range(in_ref.shape[0])]
    return jnp.concatenate(blocks + [group_ref[partner]], 1)


def spread_cams(owned, first, second):
    row = lax.broadcasted_iota(jnp.int32, owned.shape, 0)
    return owned * jnp.where(row < 9, first, jnp.where(row < 18, second, 0.0))


def halves(sums):
    return sums[0:9] + sums[9:18]


def apply_cams(owned, values, chosen):
    twice = jnp.concatenate([values, values, jnp.zeros((6, 128), F32)], 0)
    product = owned * fetch(twice, chosen)
    row = lax.broadcasted_iota(jnp.int32, (8, owned.shape[1]), 0)
    middle = product[8:16]
    first = col_sum(product[0:8] + jnp.where(row == 0, middle, 0.0))
    second = col_sum(product[16:24] + jnp.where(row == 0, 0.0, middle))
    return first, second


def start_kernel(
    partner_ref, pay_in_ref, pay_group_ref, damp_ref,
    in_ref, out_ref, rem_ref, dir_ref, pre_ref,
):
    owned = cam_rows_of(pay_in_ref, pay_group_ref, partner_ref[0])
    chosen = one_hot(owned[20:21].astype(jnp.int32), 128)
    row = lax.broadcasted_iota(jnp.int32, owned.shape, 0)
    squares = jnp.where(row < 18, owned * owned, 0.0)
    terms = jnp.concatenate([spread_cams(owned, owned[18:19], owned[19:20]), squares], 0)
    sums = collect(terms, chosen)
    remainder = -halves(sums[0:24])
    precond = 1.0 / (damp_ref[...] + halves(sums[24:48]))
    direction = precond * remainder
    rem_ref[...] = remainder
    pre_ref[...] = precond
    dir_ref[...] = direction
    first, second = apply_cams(owned, direction, chosen)
    put_payload(in_ref, out_ref, first, second, col_sum(remainder * direction))


def point_first_kernel(
    partner_ref, got_in_ref, got_group_ref, placed_ref, point_id_ref, inverse_ref,
    cam_damp_ref, dir_ref,
    in_ref, out_ref, moved_ref, norm_ref,
):
    partner = partner_ref[0]
    first = row_of(got_in_ref, got_group_ref, partner, 0)
    second = row_of(got_in_ref, got_group_ref, partner, 1)
    moved_ref[0:1, :] = first
    moved_ref[1:2, :] = second
    norm_ref[...] = jnp.broadcast_to(group_total(got_group_ref), (1, 128))
    direction = dir_ref[...]
    point_side(
        placed_ref, point_id_ref, inverse_ref, cam_damp_ref, direction, first, second, in_ref, out_ref
    )


def point_next_kernel(
    partner_ref, got_in_ref, got_group_ref, placed_ref, point_id_ref, inverse_ref,
    cam_damp_ref, dir_ref, scaled_ref, moved_ref, norm_ref,
    in_ref, out_ref, next_dir_ref, next_norm_ref,
):
    partner = partner_ref[0]
    norm_next = group_total(got_group_ref)
    ratio = norm_next / norm_ref[0:1, 0:1]
    first = row_of(got_in_ref, got_group_ref, partner, 0) + ratio * moved_ref[0:1, :]
    second = row_of(got_in_ref, got_group_ref, partner, 1) + ratio * moved_ref[1:2, :]
    direction = scaled_ref[...] + ratio * dir_ref[...]
    next_dir_ref[...] = direction
    next_norm_ref[...] = jnp.broadcast_to(norm_next, (1, 128))
    point_side(
        placed_ref, point_id_ref, inverse_ref, cam_damp_ref, direction, first, second, in_ref, out_ref
    )


def point_side(
    placed_ref, point_id_ref, inverse_ref, cam_damp_ref, direction, first, second, in_ref, out_ref
):
    placed = placed_ref[...]
    chosen = one_hot(jnp.bitwise_and(point_id_ref[...], 127), 128)
    sums = collect(spread_points(placed, first, second), chosen)
    pulled = fetch(solve_points(inverse_ref[...], sums), chosen)
    kept0, kept1 = pull_points(placed, pulled, first, second)
    bend = lane_blocks(first * kept0 + second * kept1)
    bend = bend + col_sum(cam_damp_ref[...] * direction * direction)
    put_payload(in_ref, out_ref, kept0, kept1, bend)


def image_of(partner, got_in_ref, got_group_ref, owned, chosen, damp, direction):
    first = row_of(got_in_ref, got_group_ref, partner, 0)
    second = row_of(got_in_ref, got_group_ref, partner, 1)
    return damp * direction + halves(collect(spread_cams(owned, first, second), chosen))


def camera_kernel(
    partner_ref, got_in_ref, got_group_ref, pay_in_ref, pay_group_ref,
    damp_ref, dir_ref, rem_ref, pre_ref, norm_ref,
    in_ref, out_ref, update_ref, next_rem_ref, scaled_ref,
):
    partner = partner_ref[0]
    owned = cam_rows_of(pay_in_ref, pay_group_ref, partner)
    chosen = one_hot(owned[20:21].astype(jnp.int32), 128)
    direction = dir_ref[...]
    image = image_of(
        partner, got_in_ref, got_group_ref, owned, chosen, damp_ref[...], direction
    )
    step = norm_ref[0:1, 0:1] / group_total(got_group_ref)
    remainder = rem_ref[...] - step * image
    scaled = pre_ref[...] * remainder
    update_ref[...] = step * direction
    next_rem_ref[...] = remainder
    scaled_ref[...] = scaled
    first, second = apply_cams(owned, scaled, chosen)
    put_payload(in_ref, out_ref, first, second, col_sum(remainder * scaled))


def last_kernel(
    partner_ref, got_in_ref, got_group_ref, pay_in_ref, pay_group_ref,
    damp_ref, dir_ref, rem_ref, update_ref, norm_ref,
    next_update_ref, next_rem_ref,
):
    partner = partner_ref[0]
    owned = cam_rows_of(pay_in_ref, pay_group_ref, partner)
    chosen = one_hot(owned[20:21].astype(jnp.int32), 128)
    direction = dir_ref[...]
    image = image_of(
        partner, got_in_ref, got_group_ref, owned, chosen, damp_ref[...], direction
    )
    step = norm_ref[0:1, 0:1] / group_total(got_group_ref)
    next_update_ref[...] = update_ref[...] + step * direction
    next_rem_ref[...] = rem_ref[...] - step * image


def pair_kernel(got_ref, outer_ref, pair_ref):
    partial = lane_blocks(got_ref[2:3, :])
    for i in range(pair_ref.shape[0]):
        pair_ref[i, 0:2, :] = outer_ref[...]
        pair_ref[i, 2:3, :] = partial


def call(kernel, name, smem, shapes, *args):
    vmem = pl.BlockSpec(memory_space=pltpu.VMEM)
    scalar = pl.BlockSpec(memory_space=pltpu.SMEM)
    return pl.pallas_call(
        kernel,
        name=name,
        out_shape=[jax.ShapeDtypeStruct(shape, F32) for shape in shapes],
        in_specs=[scalar] * smem + [vmem] * (len(args) - smem),
        out_specs=[vmem] * len(shapes),
        compiler_params=pltpu.CompilerParams(vmem_limit_bytes=32 * 1024 * 1024),
    )(*args)


def exchange(inner, outer):
    got = lax.all_to_all(inner, "dev", split_axis=1, concat_axis=1, tiled=True)
    (pair,) = call(pair_kernel, "pair", 0, [(lax.axis_size("group"), 3, 128)], got, outer)
    return got, lax.all_to_all(pair, "group", split_axis=0, concat_axis=0, tiled=True)


def on_device(
    cam_jac, point_jac, residuals, obs_camera, obs_point, obs_count, cam_damp, pt_damp, partner_mask
):
    n = cam_jac.shape[1]
    inner = n - 128
    groups = lax.axis_size("group")
    partner = jnp.bitwise_xor(partner_mask, lax.axis_index("group").astype(jnp.int32))
    point_ids = obs_point[None]
    pay_in, pay_group, placed, inverse = call(
        setup_kernel, "setup", 1,
        [(inner // 128, 24, 128), (groups, 24, 128), (48, n), (48, 128)],
        obs_count, cam_jac, point_jac, residuals, obs_camera[None], point_ids, pt_damp,
    )
    pay_in = lax.all_to_all(pay_in, "dev", split_axis=0, concat_axis=0, tiled=True)
    pay_group = lax.all_to_all(pay_group, "group", split_axis=0, concat_axis=0, tiled=True)
    field = (9, 128)
    payload = [(3, inner), (2, 128)]
    to_in, to_out, remainder, direction, precond = call(
        start_kernel, "start", 1, payload + [field] * 3, partner, pay_in, pay_group, cam_damp
    )
    got_in, got_group = exchange(to_in, to_out)
    to_in, to_out, moved, norm = call(
        point_first_kernel, "point_first", 1, payload + [(2, n), (1, 128)],
        partner, got_in, got_group, placed, point_ids, inverse, cam_damp, direction,
    )
    got_in, got_group = exchange(to_in, to_out)
    to_in, to_out, update, remainder, scaled = call(
        camera_kernel, "camera", 1, payload + [field] * 3,
        partner, got_in, got_group, pay_in, pay_group, cam_damp, direction, remainder, precond, norm,
    )
    got_in, got_group = exchange(to_in, to_out)
    to_in, to_out, direction, norm = call(
        point_next_kernel, "point_next", 1, payload + [field, (1, 128)],
        partner, got_in, got_group, placed, point_ids, inverse, cam_damp, direction, scaled, moved, norm,
    )
    got_in, got_group = exchange(to_in, to_out)
    update, remainder = call(
        last_kernel, "last", 1, [field] * 2,
        partner, got_in, got_group, pay_in, pay_group, cam_damp, direction, remainder, update, norm,
    )
    return (update, remainder)


def solution(mesh):
    slots, rows = P(None, ("group", "dev")), P(("group", "dev"))
    return jax.shard_map(
        on_device,
        mesh=mesh,
        in_specs=(
            slots, slots, slots, rows, rows, P(("group", "dev"), None), slots, slots, P("dev"),
        ),
        out_specs=(slots, slots),
        check_vma=False,
    )
```

time: 873 us -> 185 us (0.21)
  other arithmetic: 254 us -> 0 us
  blocking collectives: 300 us -> 124 us
  starting transfers between devices: 122 us -> 17.3 us
  local copies, waits for them, and re-layouts: 99.9 us -> 3.36 us
  waiting for transfers between devices: 81.4 us -> 27.3 us
  Pallas kernels: 0 us -> 10.2 us
    psum x3 -> x0, blocking collectives: 300 us -> none  [the longest x1 102 us: on_device(): norm_now = lax.psum(jnp.sum(remainder * scaled), ('group', 'dev'))]
    scatter-add x8 -> x0, other arithmetic: 225 us -> none  [seg_rows(): jax.ops.segment_sum(single, indices, num_segments=item_count)]
    all_to_all x0 -> x9, blocking collectives: none -> 124 us  [the longest x4 72.4 us: exchange(): got = lax.all_to_all(inner, 'dev', split_axis=1, concat_axis=1, tiled=True)]
    ppermute x20 -> x0, starting transfers between devices: 66 us -> none  [partner_2(): return lax.ppermute(block, axis, route)]
    gather x5 -> x0, local copies, waits for them, and re-layouts: 44.4 us -> none  [the longest x3 26.9 us: point_side(): return moved - point_apply(point_rows, pulled[:, obs_point])]
    all_to_all x5 -> x1, starting transfers between devices: 56.4 us -> 17.3 us  [on_device(): lax.all_to_all(pay_in, 'dev', split_axis=0, concat_axis=0, tiled=True)]
    all_to_all x5 -> x1, waiting for transfers between devices: 55.3 us -> 27.3 us  [on_device(): lax.all_to_all(pay_in, 'dev', split_axis=0, concat_axis=0, tiled=True)]
    slice x16 -> x0, local copies, waits for them, and re-layouts: 27.2 us -> none  [the longest x3 12 us: point_blocks(): point_rows[second_axis]]
  transfers between devices with their start and end apart: 25 -> 1, of which waited for: 21 -> 1; matrix products, arithmetic and copies ran while one was open for 0% -> 0% of each run, Pallas kernels for 0% -> 0%
where the time goes in v1:
time: 185 us; the launch traced here: 183 us
  blocking collectives  124 us (67%)
  waiting for transfers between devices  27.3 us (15%)
  starting transfers between devices  17.3 us (9%)
  Pallas kernels  10.2 us (6%)
  local copies, waits for them, and re-layouts  3.36 us (2%)
    all_to_all x4, blocking collectives, exchange(): got = lax.all_to_all(inner, 'dev', split_axis=1, concat_axis=1, tiled=True)  72.4 us
    all_to_all x4, blocking collectives, exchange(): lax.all_to_all(pair, 'group', split_axis=0, concat_axis=0, tiled=True)  36.9 us
    all_to_all x1, waiting for transfers between devices, on_device(): lax.all_to_all(pay_in, 'dev', split_axis=0, concat_axis=0, tiled=True)  27.3 us
    all_to_all x1, starting transfers between devices, on_device(): lax.all_to_all(pay_in, 'dev', split_axis=0, concat_axis=0, tiled=True)  17.3 us
    all_to_all x1, blocking collectives, on_device(): lax.all_to_all(pay_group, 'group', split_axis=0, concat_axis=0, tiled=True)  14.6 us
    pallas_call x10, Pallas kernels, call(): pl.pallas_call(kernel, name=name, out_shape=[jax.ShapeDtypeStruct(shape,...  10.2 us
  transfers between devices with their start and end apart: 1, of which 1 were waited for; matrix products, arithmetic and copies ran while one was open for 0% of the time, Pallas kernels for 0%

profile of v1, /device:TPU:1, one launch (start us, length us, event | category | flops | bytes accessed | tf_op | source)
XLA Modules:
  0.0 183.4 jit_solution(16216677197599212367)
XLA Ops:
  0.6 0.0 copy-start.6
  0.6 0.0 copy-start.3
  0.7 0.8 broadcast_in_dim.7.point_id_ref
  1.4 0.0 copy-done.6
  1.4 0.0 copy-start.4
  1.4 0.0 copy-start.5
  1.5 0.0 copy-done.3
  1.5 0.7 copy-done.4
  2.1 0.0 copy-done.5
  2.1 0.0 copy-start
  2.1 1.0 copy-done
  3.1 0.0 copy-start.2
  3.1 0.9 copy-done.2
  4.0 3.2 %setup.1 = (f32[32,24,128]{2,1,0:T(8,128)}, f32[16,24,128]{2,1,0:T(8,128)S(1)}, f32[48,4224]{1,0:T(8,128)S(1)}, f32[48,128]{1,0:T(8,128)S(1)}) custom-call(s32[1,33]{1,0:T(1,128)S(1)} %copy-done.5, f32[18,4224]{1,0:T(8,128)S(1)} %copy-done, f32[6,4224]{1,0:T(8,128)S(1)} %copy-done.2, f32[2,4224]{1,0:T(2,128)S(1)} %copy-done.3, ...), custom_call_target="tpu_custom_call" | custom-call | tf_op jit(solution)/shard_map/setup/pallas_call | solution.py:314
  7.3 14.6 %all_to_all.74.pay_group_ref = f32[16,24,128]{2,1,0:T(8,128)S(1)} all-to-all(f32[16,24,128]{2,1,0:T(8,128)S(1)} %get-tuple-element.25), channel_id=1, replica_groups=mesh['group'=16,'dev'=32] {'group'}, dimensions={0} | all-to-all | bytes 393216 | tf_op jit(solution)/shard_map/all_to_all | solution.py:344
  21.9 17.3 %all-to-all-start = ((f32[32,24,128]{2,1,0:T(8,128)}), f32[32,24,128]{2,1,0:T(8,128)S(1)}, u32[]{:S(2)}, u32[]{:S(2)}) async-start(f32[32,24,128]{2,1,0:T(8,128)} %get-tuple-element.24), calls=%async_computation | async-start | bytes 786432 | tf_op jit(solution)/shard_map/all_to_all | solution.py:343
  39.2 0.0 copy-start.1
  39.9 27.3 %all-to-all-done.pay_in_ref = f32[32,24,128]{2,1,0:T(8,128)S(1)} async-done(((f32[32,24,128]{2,1,0:T(8,128)}), f32[32,24,128]{2,1,0:T(8,128)S(1)}, u32[]{:S(2)}, u32[]{:S(2)}) %all-to-all-start) | async-done | bytes 393248 | tf_op jit(solution)/shard_map/all_to_all | solution.py:343
  67.2 0.0 copy-done.1
  67.2 1.3 start.1
  68.5 16.2 %all_to_all.75 = f32[3,32,128]{2,0,1:T(4,128)S(1)} all-to-all(f32[3,32,128]{2,0,1:T(4,128)S(1)} %bitcast.20), channel_id=1, replica_groups=mesh['group'=16,'dev'=32] {'dev'}, dimensions={1} | all-to-all | bytes 98304 | tf_op jit(solution)/shard_map/all_to_all | solution.py:325
  84.8 9.2 %all_to_all.76.got_group_ref = f32[16,3,128]{2,1,0:T(4,128)S(1)} all-to-all(f32[16,3,128]{2,1,0:T(4,128)S(1)} %pair.4), channel_id=1, replica_groups=mesh['group'=16,'dev'=32] {'group'}, dimensions={0} | all-to-all | bytes 49152 | tf_op jit(solution)/shard_map/all_to_all | solution.py:327
  93.9 1.4 point_first.1
  95.3 18.7 %all_to_all.77 = f32[3,32,128]{2,0,1:T(4,128)S(1)} all-to-all(f32[3,32,128]{2,0,1:T(4,128)S(1)} %bitcast.19), channel_id=1, replica_groups=mesh['group'=16,'dev'=32] {'dev'}, dimensions={1} | all-to-all | bytes 98304 | tf_op jit(solution)/shard_map/all_to_all | solution.py:325
  114.1 9.2 %all_to_all.78.got_group_ref = f32[16,3,128]{2,1,0:T(4,128)S(1)} all-to-all(f32[16,3,128]{2,1,0:T(4,128)S(1)} %pair.5), channel_id=1, replica_groups=mesh['group'=16,'dev'=32] {'group'}, dimensions={0} | all-to-all | bytes 49152 | tf_op jit(solution)/shard_map/all_to_all | solution.py:327
  123.3 1.4 camera.1
  124.7 18.7 %all_to_all.79 = f32[3,32,128]{2,0,1:T(4,128)S(1)} all-to-all(f32[3,32,128]{2,0,1:T(4,128)S(1)} %bitcast.18), channel_id=1, replica_groups=mesh['group'=16,'dev'=32] {'dev'}, dimensions={1} | all-to-all | bytes 98304 | tf_op jit(solution)/shard_map/all_to_all | solution.py:325
  143.5 9.2 %all_to_all.80.got_group_ref = f32[16,3,128]{2,1,0:T(4,128)S(1)} all-to-all(f32[16,3,128]{2,1,0:T(4,128)S(1)} %pair.6), channel_id=1, replica_groups=mesh['group'=16,'dev'=32] {'group'}, dimensions={0} | all-to-all | bytes 49152 | tf_op jit(solution)/shard_map/all_to_all | solution.py:327
  152.7 1.6 point_next.1
  154.3 18.7 %all_to_all.81 = f32[3,32,128]{2,0,1:T(4,128)S(1)} all-to-all(f32[3,32,128]{2,0,1:T(4,128)S(1)} %bitcast.17), channel_id=1, replica_groups=mesh['group'=16,'dev'=32] {'dev'}, dimensions={1} | all-to-all | bytes 98304 | tf_op jit(solution)/shard_map/all_to_all | solution.py:325
  173.0 9.2 %all_to_all.82.got_group_ref = f32[16,3,128]{2,1,0:T(4,128)S(1)} all-to-all(f32[16,3,128]{2,1,0:T(4,128)S(1)} %pair.7), channel_id=1, replica_groups=mesh['group'=16,'dev'=32] {'group'}, dimensions={0} | all-to-all | bytes 49152 | tf_op jit(solution)/shard_map/all_to_all | solution.py:327
  182.3 1.1 last.1
  (5 shorter events, 0.2 us)
Async XLA Ops:
  0.6 0.8 copy-start.6
  0.6 0.8 copy-start.3
  1.4 0.7 copy-start.4
  1.4 0.7 copy-start.5
  2.1 1.0 copy-start
  3.1 0.9 copy-start.2
  21.9 45.3 %all-to-all-start = ((f32[32,24,128]{2,1,0:T(8,128)}), f32[32,24,128]{2,1,0:T(8,128)S(1)}, u32[]{:S(2)}, u32[]{:S(2)}) async-start(f32[32,24,128]{2,1,0:T(8,128)} %get-tuple-element.24), calls=%async_computation | async-start | bytes 786432 | tf_op jit(solution)/shard_map/all_to_all | solution.py:343
  39.2 28.0 %copy-start.1 = (f32[9,128]{1,0:T(8,128)S(1)}, f32[9,128]{1,0:T(8,128)}, u32[]{:S(2)}) copy-start(f32[9,128]{1,0:T(8,128)} %damp_ref.7) | copy-start | bytes 13828

commit v2 on v1

v2 whole, which is shorter than its diff:
```python
import jax
import jax.numpy as jnp
from jax import lax
from jax.experimental import pallas as pl
from jax.experimental.pallas import tpu as pltpu
from jax.sharding import PartitionSpec as P

F32 = jnp.float32
BF16 = jnp.bfloat16
PAIRS = ((0, 0), (0, 1), (0, 2), (1, 1), (1, 2), (2, 2))


def one_hot(ids, count):
    rows = lax.broadcasted_iota(jnp.int32, (count, ids.shape[1]), 0)
    return jnp.where(rows == ids, 1.0, 0.0).astype(BF16)


def pieces(values, count):
    found = []
    for _ in range(count - 1):
        found.append(values.astype(BF16).astype(F32))
        values = values - found[-1]
    return found + [values]


def collect(values, chosen, count=2):
    m = values.shape[0]
    stacked = jnp.concatenate(pieces(values, count), 0).astype(BF16)
    sums = lax.dot_general(
        stacked, chosen, (((1,), (1,)), ((), ())), preferred_element_type=F32
    )
    total = sums[0:m]
    for i in range(1, count):
        total = total + sums[i * m : (i + 1) * m]
    return total


def fetch(items, chosen):
    stacked = jnp.concatenate(pieces(items, 2), 1).astype(BF16)
    return jnp.dot(
        stacked, jnp.concatenate([chosen, chosen], 0), preferred_element_type=F32
    )


def col_sum(values):
    return jnp.sum(values, axis=0, keepdims=True)


def total(values):
    return jnp.sum(values, keepdims=True)


def lane_blocks(row):
    out = row[:, 0:128]
    for b in range(1, row.shape[1] // 128):
        out = out + row[:, b * 128 : (b + 1) * 128]
    return out


def scalar_row(values):
    lanes = lax.broadcasted_iota(jnp.int32, (1, 128), 1)
    row = jnp.broadcast_to(values[0], (1, 128))
    for i in range(1, len(values)):
        row = jnp.where(lanes < 32 * i, row, values[i])
    return row


def scalars(row, count):
    return [row[:, 32 * i : 32 * i + 1] for i in range(count)]


def put_rows(ref, rows):
    for r, row in enumerate(rows):
        ref[r : r + 1, :] = row


def repeat(row, width):
    return jnp.concatenate([row] * (width // 128), 1)


def with_outer(in_ref, out_ref, r):
    return jnp.concatenate([in_ref[r : r + 1, :], out_ref[r : r + 1, :]], 1)


def solve_points(inverse, sums):
    c = [inverse[8 * i : 8 * i + 8] for i in range(6)]
    g = [sums[8 * i : 8 * i + 8] for i in range(3)]
    return jnp.concatenate(
        [
            c[0] * g[0] + c[1] * g[1] + c[2] * g[2],
            c[1] * g[0] + c[3] * g[1] + c[4] * g[2],
            c[2] * g[0] + c[4] * g[1] + c[5] * g[2],
        ],
        0,
    )


def spread_points(placed, first, second):
    return jnp.concatenate(
        [
            placed[8 * r : 8 * r + 8] * first + placed[24 + 8 * r : 32 + 8 * r] * second
            for r in range(3)
        ],
        0,
    )


def pull_points(placed, pulled, first, second):
    v0 = placed[0:8] * pulled[0:8] + placed[8:16] * pulled[8:16] + placed[16:24] * pulled[16:24]
    v1 = placed[24:32] * pulled[0:8] + placed[32:40] * pulled[8:16] + placed[40:48] * pulled[16:24]
    return first - col_sum(v0), second - col_sum(v1)


def setup_kernel(
    count_ref, cam_ref, point_ref, res_ref, cam_id_ref, point_id_ref, damp_ref,
    in_ref, outer_ref, outer_sum_ref, placed_ref, inverse_ref,
):
    n = cam_ref.shape[1]
    inner = n - 128
    lanes = lax.broadcasted_iota(jnp.int32, (1, 128), 1)
    live = jnp.concatenate(
        [jnp.where(lanes < count_ref[0, b], 1.0, 0.0) for b in range(n // 128)], 1
    )
    ids = point_id_ref[...]
    chosen = one_hot(jnp.bitwise_and(ids, 127), 128)
    high = jnp.right_shift(ids, 7)
    digit = jnp.where(lax.broadcasted_iota(jnp.int32, (8, n), 0) == high, live, 0.0)
    for r in range(6):
        placed_ref[8 * r : 8 * r + 8, :] = digit * point_ref[r : r + 1, :]
    placed = placed_ref[...]
    part = [placed[8 * r : 8 * r + 8] for r in range(6)]
    first, second = res_ref[0:1, :], res_ref[1:2, :]
    squares = [part[a] * part[b] + part[3 + a] * part[3 + b] for a, b in PAIRS]
    blocks = collect(jnp.concatenate(squares, 0), chosen, 3)
    sums = collect(spread_points(placed, first, second), chosen)
    b = [blocks[8 * i : 8 * i + 8] for i in range(6)]
    for axis, entry in ((0, 0), (1, 3), (2, 5)):
        damp = damp_ref[axis : axis + 1, :]
        b[entry] = b[entry] + jnp.concatenate(
            [damp[:, 128 * h : 128 * h + 128] for h in range(8)], 0
        )
    cof = [
        b[3] * b[5] - b[4] * b[4],
        b[2] * b[4] - b[1] * b[5],
        b[1] * b[4] - b[2] * b[3],
        b[0] * b[5] - b[2] * b[2],
        b[1] * b[2] - b[0] * b[4],
        b[0] * b[3] - b[1] * b[1],
    ]
    det = b[0] * cof[0] + b[1] * cof[1] + b[2] * cof[2]
    inverse = jnp.concatenate([c / det for c in cof], 0)
    inverse_ref[...] = inverse
    pulled = fetch(solve_points(inverse, sums), chosen)
    first, second = pull_points(placed, pulled, first, second)
    rows = cam_ref[...] * live
    cam_ids = cam_id_ref[...].astype(F32)

    def put(ref, lo):
        hi = lo + 128
        ref[0:18, :] = rows[:, lo:hi]
        ref[18:19, :] = first[:, lo:hi]
        ref[19:20, :] = second[:, lo:hi]
        ref[20:21, :] = cam_ids[:, lo:hi]
        ref[21:24, :] = jnp.zeros((3, 128), F32)

    for i in range(in_ref.shape[0]):
        put(in_ref.at[i], 128 * i)
    put(outer_ref, inner)
    outer_sum_ref[...] = start_sums(outer_ref[...])


def spread_cams(owned, first, second):
    row = lax.broadcasted_iota(jnp.int32, owned.shape, 0)
    return owned * jnp.where(row < 9, first, jnp.where(row < 18, second, 0.0))


def halves(sums):
    return sums[0:9] + sums[9:18]


def apply_cams(owned, values, chosen):
    twice = jnp.concatenate([values, values, jnp.zeros((6, 128), F32)], 0)
    product = owned * fetch(twice, chosen)
    row = lax.broadcasted_iota(jnp.int32, (8, owned.shape[1]), 0)
    middle = product[8:16]
    first = col_sum(product[0:8] + jnp.where(row == 0, middle, 0.0))
    second = col_sum(product[16:24] + jnp.where(row == 0, 0.0, middle))
    return first, second


def ids_of(owned):
    return one_hot(owned[20:21].astype(jnp.int32), 128)


def start_sums(owned):
    row = lax.broadcasted_iota(jnp.int32, owned.shape, 0)
    squares = jnp.where(row < 18, owned * owned, 0.0)
    terms = jnp.concatenate([spread_cams(owned, owned[18:19], owned[19:20]), squares], 0)
    sums = collect(terms, ids_of(owned))
    return jnp.concatenate([halves(sums[0:24]), halves(sums[24:48])], 0)


def blocks_of(pay_ref):
    return jnp.concatenate([pay_ref[i] for i in range(pay_ref.shape[0])], 1)


def start_sum_kernel(pay_ref, outer_sum_ref, damp_ref, group_ref):
    sums = start_sums(blocks_of(pay_ref))
    for i in range(group_ref.shape[0]):
        group_ref[i, 0:9, :] = sums[0:9]
        group_ref[i, 9:18, :] = sums[9:18] + damp_ref[...]
        group_ref[i, 18:36, :] = outer_sum_ref[...]


def put_moved(in_ref, out_ref, pay_ref, outer_ref, own, twin):
    owned = blocks_of(pay_ref)
    put_rows(in_ref, apply_cams(owned, own, ids_of(owned)))
    outer = outer_ref[...]
    put_rows(out_ref, apply_cams(outer, twin, ids_of(outer)))


def start_kernel(
    partner_ref, group_ref, outer_sum_ref, pay_ref, outer_ref,
    in_ref, out_ref, rem_ref, pre_ref, dir_ref,
):
    theirs = group_ref[partner_ref[0]]
    mine = group_ref[partner_ref[1]]
    sums = [mine[0:18] + theirs[18:36], theirs[0:18] + outer_sum_ref[...]]
    for i in range(2):
        remainder = -sums[i][0:9]
        precond = 1.0 / sums[i][9:18]
        rem_ref[i] = remainder
        pre_ref[i] = precond
        dir_ref[i] = precond * remainder
    put_moved(in_ref, out_ref, pay_ref, outer_ref, dir_ref[0], dir_ref[1])


def point_side(in_ref, out_ref, placed_ref, point_id_ref, inverse_ref):
    placed = placed_ref[...]
    first, second = with_outer(in_ref, out_ref, 0), with_outer(in_ref, out_ref, 1)
    chosen = one_hot(jnp.bitwise_and(point_id_ref[...], 127), 128)
    sums = collect(spread_points(placed, first, second), chosen)
    pulled = fetch(solve_points(inverse_ref[...], sums), chosen)
    kept = pull_points(placed, pulled, first, second)
    return kept, total(lane_blocks(first * kept[0] + second * kept[1]))


def put_kept(back_ref, outer_sum_ref, outer_ref, kept, values):
    inner = back_ref.shape[1]
    put_rows(back_ref, [kept[0][:, :inner], kept[1][:, :inner], repeat(scalar_row(values), inner)])
    outer = outer_ref[...]
    spread = spread_cams(outer, kept[0][:, inner:], kept[1][:, inner:])
    outer_sum_ref[...] = halves(collect(spread, ids_of(outer)))


def point_first_kernel(
    in_ref, out_ref, placed_ref, point_id_ref, inverse_ref, outer_ref, damp_ref, rem_ref, dir_ref,
    back_ref, outer_sum_ref,
):
    kept, bend = point_side(in_ref, out_ref, placed_ref, point_id_ref, inverse_ref)
    direction = dir_ref[0]
    bend = bend + total(damp_ref[...] * direction * direction)
    put_kept(back_ref, outer_sum_ref, outer_ref, kept, [total(rem_ref[0] * direction), bend])


def point_next_kernel(
    in_ref, out_ref, placed_ref, point_id_ref, inverse_ref, outer_ref, damp_ref,
    rem_ref, scaled_ref, image_ref,
    back_ref, outer_sum_ref,
):
    kept, bend = point_side(in_ref, out_ref, placed_ref, point_id_ref, inverse_ref)
    scaled = scaled_ref[0]
    bend = bend + total(damp_ref[...] * scaled * scaled)
    values = [total(rem_ref[0] * scaled), bend, total(image_ref[...] * scaled)]
    put_kept(back_ref, outer_sum_ref, outer_ref, kept, values)


def inner_image(back_ref, pay_ref, damp_ref, field):
    owned = blocks_of(pay_ref)
    spread = spread_cams(owned, back_ref[0:1, :], back_ref[1:2, :])
    return damp_ref[...] * field + halves(collect(spread, ids_of(owned)))


def image_kernel(back_ref, outer_sum_ref, pay_ref, damp_ref, dir_ref, group_ref):
    image = inner_image(back_ref, pay_ref, damp_ref, dir_ref[0])
    partial = lane_blocks(back_ref[2:3, :])
    for i in range(group_ref.shape[0]):
        group_ref[i, 0:9, :] = image
        group_ref[i, 9:18, :] = outer_sum_ref[...]
        group_ref[i, 18:19, :] = partial


def group_total(group_ref, r):
    row = group_ref[0, r : r + 1, :]
    for i in range(1, group_ref.shape[0]):
        row = row + group_ref[i, r : r + 1, :]
    return row


def camera_kernel(
    partner_ref, group_ref, outer_sum_ref, pay_ref, outer_ref, rem_ref, pre_ref, dir_ref,
    in_ref, out_ref, next_rem_ref, scaled_ref, image_ref, sums_ref,
):
    sums = group_total(group_ref, 18)
    sums_ref[...] = sums
    norm, bend = scalars(sums, 2)
    step = norm / bend
    theirs = group_ref[partner_ref[0]]
    mine = group_ref[partner_ref[1]]
    images = [mine[0:9] + theirs[9:18], theirs[0:9] + outer_sum_ref[...]]
    image_ref[...] = images[0]
    for i in range(2):
        remainder = rem_ref[i] - step * images[i]
        next_rem_ref[i] = remainder
        scaled_ref[i] = pre_ref[i] * remainder
    put_moved(in_ref, out_ref, pay_ref, outer_ref, scaled_ref[0], scaled_ref[1])


def pair_kernel(back_ref, outer_sum_ref, group_ref):
    partial = lane_blocks(back_ref[2:3, :])
    for i in range(group_ref.shape[0]):
        group_ref[i, 0:9, :] = outer_sum_ref[...]
        group_ref[i, 9:10, :] = partial


def inner_kernel(back_ref, pay_ref, damp_ref, scaled_ref, image_ref):
    image_ref[...] = inner_image(back_ref, pay_ref, damp_ref, scaled_ref[0])


def last_kernel(
    partner_ref, group_ref, inner_ref, rem_ref, scaled_ref, dir_ref, image_ref, sums_ref,
    update_ref, next_rem_ref,
):
    norm, bend = scalars(sums_ref[...], 2)
    next_norm, next_bend, cross = scalars(group_total(group_ref, 9), 3)
    ratio = next_norm / norm
    next_bend = next_bend + ratio * (2.0 * cross + ratio * bend)
    step = next_norm / next_bend
    image = inner_ref[...] + group_ref[partner_ref[0], 0:9, :] + ratio * image_ref[...]
    direction = dir_ref[0]
    update_ref[...] = norm / bend * direction + step * (scaled_ref[0] + ratio * direction)
    next_rem_ref[...] = rem_ref[0] - step * image


def call(kernel, name, smem, shapes, *args):
    vmem = pl.BlockSpec(memory_space=pltpu.VMEM)
    scalar = pl.BlockSpec(memory_space=pltpu.SMEM)
    return pl.pallas_call(
        kernel,
        name=name,
        out_shape=[jax.ShapeDtypeStruct(shape, F32) for shape in shapes],
        in_specs=[scalar] * smem + [vmem] * (len(args) - smem),
        out_specs=[vmem] * len(shapes),
        compiler_params=pltpu.CompilerParams(vmem_limit_bytes=32 * 1024 * 1024),
    )(*args)


def on_device(
    cam_jac, point_jac, residuals, obs_camera, obs_point, obs_count, cam_damp, pt_damp, partner_mask
):
    n = cam_jac.shape[1]
    inner = n - 128
    groups = lax.axis_size("group")
    own = lax.axis_index("group").astype(jnp.int32)
    partner = jnp.stack([jnp.bitwise_xor(partner_mask[0], own), own])
    point_ids = obs_point[None]

    def over_dev(values, axis=1):
        return lax.all_to_all(values, "dev", split_axis=axis, concat_axis=axis, tiled=True)

    def over_group(values):
        return lax.all_to_all(values, "group", split_axis=0, concat_axis=0, tiled=True)

    field, fields, pair, back = (9, 128), (2, 9, 128), [(2, inner), (2, 128)], (3, inner)
    pay, outer, outer_sum, placed, inverse = call(
        setup_kernel, "setup", 1,
        [(inner // 128, 24, 128), (24, 128), (18, 128), (48, n), (48, 128)],
        obs_count, cam_jac, point_jac, residuals, obs_camera[None], point_ids, pt_damp,
    )
    pay = over_dev(pay, 0)
    (sums,) = call(
        start_sum_kernel, "start_sum", 0, [(groups, 36, 128)], pay, outer_sum, cam_damp
    )
    moved, outer_moved, remainder, precond, direction = call(
        start_kernel, "start", 1, pair + [fields] * 3,
        partner, over_group(sums), outer_sum, pay, outer,
    )
    points = (placed, point_ids, inverse, outer, cam_damp)
    kept, outer_sum = call(
        point_first_kernel, "point_first", 0, [back, field],
        over_dev(moved), outer_moved, *points, remainder, direction,
    )
    kept = over_dev(kept)
    (images,) = call(
        image_kernel, "image", 0, [(groups, 19, 128)], kept, outer_sum, pay, cam_damp, direction
    )
    moved, outer_moved, remainder, scaled, image, totals = call(
        camera_kernel, "camera", 1, pair + [fields] * 2 + [field, (1, 128)],
        partner, over_group(images), outer_sum, pay, outer, remainder, precond, direction,
    )
    kept, outer_sum = call(
        point_next_kernel, "point_next", 0, [back, field],
        over_dev(moved), outer_moved, *points, remainder, scaled, image,
    )
    kept = over_dev(kept)
    (images,) = call(pair_kernel, "pair", 0, [(groups, 10, 128)], kept, outer_sum)
    (next_image,) = call(inner_kernel, "inner", 0, [field], kept, pay, cam_damp, scaled)
    update, remainder = call(
        last_kernel, "last", 1, [field] * 2,
        partner, over_group(images), next_image, remainder, scaled, direction, image, totals,
    )
    return (update, remainder)


def solution(mesh):
    slots, rows = P(None, ("group", "dev")), P(("group", "dev"))
    return jax.shard_map(
        on_device,
        mesh=mesh,
        in_specs=(
            slots, slots, slots, rows, rows, P(("group", "dev"), None), slots, slots, P("dev"),
        ),
        out_specs=(slots, slots),
        check_vma=False,
    )
```

time: 185 us -> 165 us (0.89)
  waiting for transfers between devices: 27.3 us -> 14.3 us
  starting transfers between devices: 17.3 us -> 10.3 us
  Pallas kernels: 10.2 us -> 12.3 us
  blocking collectives: 124 us -> 122 us
    all_to_all x1 -> x2, waiting for transfers between devices: 27.3 us -> 14.3 us  [over_group(): lax.all_to_all(values, 'group', split_axis=0, concat_axis=0, tiled=True)]
    all_to_all x1 -> x2, starting transfers between devices: 17.3 us -> 10.3 us  [over_group(): lax.all_to_all(values, 'group', split_axis=0, concat_axis=0, tiled=True)]
    pallas_call x10, Pallas kernels: 10.2 us -> 12.3 us  [call(): pl.pallas_call(kernel, name=name, out_shape=[jax.ShapeDtypeStruct(shape,...]
    all_to_all x9 -> x6, blocking collectives: 124 us -> 122 us  [the longest x5 112 us: over_dev(): lax.all_to_all(values, 'dev', split_axis=axis, concat_axis=axis, tiled=True)]
  transfers between devices with their start and end apart: 1 -> 2, of which waited for: 1 -> 2; matrix products, arithmetic and copies ran while one was open for 0% -> 0% of each run, Pallas kernels for 0% -> 0%
where the time goes in v2:
time: 165 us; the launch traced here: 164 us
  blocking collectives  122 us (74%)
  waiting for transfers between devices  14.3 us (9%)
  Pallas kernels  12.3 us (7%)
  starting transfers between devices  10.3 us (6%)
  local copies, waits for them, and re-layouts  3.36 us (2%)
    all_to_all x5, blocking collectives, over_dev(): lax.all_to_all(values, 'dev', split_axis=axis, concat_axis=axis, tiled=True)  112 us
    all_to_all x2, waiting for transfers between devices, over_group(): lax.all_to_all(values, 'group', split_axis=0, concat_axis=0, tiled=True)  14.3 us
    pallas_call x10, Pallas kernels, call(): pl.pallas_call(kernel, name=name, out_shape=[jax.ShapeDtypeStruct(shape,...  12.3 us
    all_to_all x2, starting transfers between devices, over_group(): lax.all_to_all(values, 'group', split_axis=0, concat_axis=0, tiled=True)  10.3 us
    all_to_all x1, blocking collectives, over_group(): lax.all_to_all(values, 'group', split_axis=0, concat_axis=0, tiled=True)  9.78 us
  transfers between devices with their start and end apart: 2, of which 2 were waited for; matrix products, arithmetic and copies ran while one was open for 0% of the time, Pallas kernels for 0%

profile of v2, /device:TPU:1, one launch (start us, length us, event | category | flops | bytes accessed | tf_op | source)
XLA Modules:
  0.0 163.9 jit_solution(13178037082792117655)
XLA Ops:
  0.6 0.0 copy-start.6
  0.6 0.0 copy-start.3
  0.7 0.8 broadcast_in_dim.7.point_id_ref
  1.4 0.0 copy-done.6
  1.4 0.0 copy-start.4
  1.4 0.0 copy-start.5
  1.5 0.0 copy-done.3
  1.5 0.7 copy-done.4
  2.1 0.0 copy-done.5
  2.1 0.0 copy-start
  2.1 1.0 copy-done
  3.1 0.0 copy-start.2
  3.1 0.9 copy-done.2
  4.0 2.5 %setup.1 = (f32[32,24,128]{2,1,0:T(8,128)S(1)}, f32[24,128]{1,0:T(8,128)S(1)}, f32[18,128]{1,0:T(8,128)S(1)}, f32[48,4224]{1,0:T(8,128)S(1)}, f32[48,128]{1,0:T(8,128)S(1)}) custom-call(s32[1,33]{1,0:T(1,128)S(1)} %copy-done.5, f32[18,4224]{1,0:T(8,128)S(1)} %copy-done, f32[6,4224]{1,0:T(8,128)S(1)} %copy-done.2, f32[2,4224]{1,0:T(2,128)S(1)} %copy-done.3, ...), custom_call_target="tpu_custom_call" | custom-call | tf_op jit(solution)/shard_map/setup/pallas_call | solution.py:348
  6.6 0.0 copy-start.1
  6.6 44.5 %all_to_all.64.pay_ref = f32[32,24,128]{2,1,0:T(8,128)S(1)} all-to-all(f32[32,24,128]{2,1,0:T(8,128)S(1)} %get-tuple-element.22), channel_id=1, replica_groups=mesh['group'=16,'dev'=32] {'dev'}, dimensions={0} | all-to-all | bytes 786432 | tf_op jit(solution)/shard_map/all_to_all | solution.py:369
  51.1 0.0 copy-done.1
  51.1 1.2 start_sum.1
  52.3 6.8 %all-to-all-start.1 = ((f32[16,36,128]{2,1,0:T(8,128)}), f32[16,36,128]{2,1,0:T(8,128)S(1)}, u32[]{:S(2)}, u32[]{:S(2)}) async-start(f32[16,36,128]{2,1,0:T(8,128)} %start_sum.1), calls=%async_computation.1 | async-start | bytes 655360 | tf_op jit(solution)/shard_map/all_to_all | solution.py:372
  59.7 0.1 pad_add_fusion.partner_ref
  59.8 7.9 %all-to-all-done.1.group_ref = f32[16,36,128]{2,1,0:T(8,128)S(1)} async-done(((f32[16,36,128]{2,1,0:T(8,128)}), f32[16,36,128]{2,1,0:T(8,128)S(1)}, u32[]{:S(2)}, u32[]{:S(2)}) %all-to-all-start.1) | async-done | bytes 294944 | tf_op jit(solution)/shard_map/all_to_all | solution.py:372
  67.8 1.1 start.1
  68.9 16.6 %all_to_all.65 = f32[2,32,128]{2,0,1:T(2,128)S(1)} all-to-all(f32[2,32,128]{2,0,1:T(2,128)S(1)} %bitcast.20), channel_id=1, replica_groups=mesh['group'=16,'dev'=32] {'dev'}, dimensions={1} | all-to-all | bytes 65536 | tf_op jit(solution)/shard_map/all_to_all | solution.py:369
  85.5 1.5 point_first.1
  87.0 16.7 %all_to_all.66 = f32[3,32,128]{2,0,1:T(4,128)S(1)} all-to-all(f32[3,32,128]{2,0,1:T(4,128)S(1)} %bitcast.18), channel_id=1, replica_groups=mesh['group'=16,'dev'=32] {'dev'}, dimensions={1} | all-to-all | bytes 98304 | tf_op jit(solution)/shard_map/all_to_all | solution.py:369
  103.7 0.5 image.1
  104.2 9.8 %all_to_all.67.group_ref = f32[16,19,128]{2,1,0:T(8,128)S(1)} all-to-all(f32[16,19,128]{2,1,0:T(8,128)S(1)} %image.1), channel_id=1, replica_groups=mesh['group'=16,'dev'=32] {'group'}, dimensions={0} | all-to-all | bytes 311296 | tf_op jit(solution)/shard_map/all_to_all | solution.py:372
  113.9 1.2 camera.1
  115.2 17.9 %all_to_all.68 = f32[2,32,128]{2,0,1:T(2,128)S(1)} all-to-all(f32[2,32,128]{2,0,1:T(2,128)S(1)} %bitcast.19), channel_id=1, replica_groups=mesh['group'=16,'dev'=32] {'dev'}, dimensions={1} | all-to-all | bytes 65536 | tf_op jit(solution)/shard_map/all_to_all | solution.py:369
  133.1 1.5 point_next.1
  134.6 16.7 %all_to_all.69 = f32[3,32,128]{2,0,1:T(4,128)S(1)} all-to-all(f32[3,32,128]{2,0,1:T(4,128)S(1)} %bitcast.17), channel_id=1, replica_groups=mesh['group'=16,'dev'=32] {'dev'}, dimensions={1} | all-to-all | bytes 98304 | tf_op jit(solution)/shard_map/all_to_all | solution.py:369
  151.3 0.7 pair.1
  152.0 3.5 %all-to-all-start.7 = ((f32[16,10,128]{2,1,0:T(8,128)}), f32[16,10,128]{2,1,0:T(8,128)S(1)}, u32[]{:S(2)}, u32[]{:S(2)}) async-start(f32[16,10,128]{2,1,0:T(8,128)} %pair.1), calls=%async_computation.7 | async-start | bytes 262144 | tf_op jit(solution)/shard_map/all_to_all | solution.py:372
  155.6 0.5 inner.1.inner_ref
  156.0 6.3 %all-to-all-done.7.group_ref = f32[16,10,128]{2,1,0:T(8,128)S(1)} async-done(((f32[16,10,128]{2,1,0:T(8,128)}), f32[16,10,128]{2,1,0:T(8,128)S(1)}, u32[]{:S(2)}, u32[]{:S(2)}) %all-to-all-start.7) | async-done | bytes 81952 | tf_op jit(solution)/shard_map/all_to_all | solution.py:372
  162.4 1.5 last.1
  (1 shorter events, 0.0 us)
Async XLA Ops:
  0.6 0.8 copy-start.6
  0.6 0.8 copy-start.3
  1.4 0.7 copy-start.4
  1.4 0.7 copy-start.5
  2.1 1.0 copy-start
  3.1 0.9 copy-start.2
  6.6 44.5 %copy-start.1 = (f32[9,128]{1,0:T(8,128)S(1)}, f32[9,128]{1,0:T(8,128)}, u32[]{:S(2)}) copy-start(f32[9,128]{1,0:T(8,128)} %damp_ref.11) | copy-start | bytes 13828
  52.3 15.4 %all-to-all-start.1 = ((f32[16,36,128]{2,1,0:T(8,128)}), f32[16,36,128]{2,1,0:T(8,128)S(1)}, u32[]{:S(2)}, u32[]{:S(2)}) async-start(f32[16,36,128]{2,1,0:T(8,128)} %start_sum.1), calls=%async_computation.1 | async-start | bytes 655360 | tf_op jit(solution)/shard_map/all_to_all | solution.py:372
  152.0 10.3 %all-to-all-start.7 = ((f32[16,10,128]{2,1,0:T(8,128)}), f32[16,10,128]{2,1,0:T(8,128)S(1)}, u32[]{:S(2)}, u32[]{:S(2)}) async-start(f32[16,10,128]{2,1,0:T(8,128)} %pair.1), calls=%async_computation.7 | async-start | bytes 262144 | tf_op jit(solution)/shard_map/all_to_all | solution.py:372

commit v3 on v2

--- a/solution.py
+++ b/solution.py
@@ -7,6 +7,7 @@
 
 F32 = jnp.float32
 BF16 = jnp.bfloat16
+ROWS = 21
 PAIRS = ((0, 0), (0, 1), (0, 2), (1, 1), (1, 2), (2, 2))
 
 
@@ -111,29 +112,46 @@
     return first - col_sum(v0), second - col_sum(v1)
 
 
-def setup_kernel(
-    count_ref, cam_ref, point_ref, res_ref, cam_id_ref, point_id_ref, damp_ref,
-    in_ref, outer_ref, outer_sum_ref, placed_ref, inverse_ref,
+def setup_kernel(*refs):
+    inputs, mask, outputs, copies, sems = refs[:7], refs[7], refs[8:15], refs[15:22], refs[22]
+    copying = [
+        pltpu.make_async_copy(source, copy, sems.at[i])
+        for i, (source, copy) in enumerate(zip(inputs, copies))
+    ]
+    for copy in copying:
+        copy.start()
+    setup(copying, *copies, mask, *outputs)
+
+
+def setup(
+    copying, point_id_ref, count_ref, point_ref, res_ref, damp_ref, cam_ref, cam_id_ref, mask_ref,
+    in_ref, outer_ref, outer_sum_ref, placed_ref, inverse_ref, ids_ref, partner_ref,
 ):
     n = cam_ref.shape[1]
     inner = n - 128
     lanes = lax.broadcasted_iota(jnp.int32, (1, 128), 1)
+    copying[1].wait()
     live = jnp.concatenate(
         [jnp.where(lanes < count_ref[0, b], 1.0, 0.0) for b in range(n // 128)], 1
     )
-    ids = point_id_ref[...]
+    copying[0].wait()
+    ids = point_id_ref[...].reshape(1, n)
+    ids_ref[...] = ids
     chosen = one_hot(jnp.bitwise_and(ids, 127), 128)
     high = jnp.right_shift(ids, 7)
     digit = jnp.where(lax.broadcasted_iota(jnp.int32, (8, n), 0) == high, live, 0.0)
+    copying[2].wait()
     for r in range(6):
         placed_ref[8 * r : 8 * r + 8, :] = digit * point_ref[r : r + 1, :]
     placed = placed_ref[...]
     part = [placed[8 * r : 8 * r + 8] for r in range(6)]
+    copying[3].wait()
     first, second = res_ref[0:1, :], res_ref[1:2, :]
     squares = [part[a] * part[b] + part[3 + a] * part[3 + b] for a, b in PAIRS]
     blocks = collect(jnp.concatenate(squares, 0), chosen, 3)
     sums = collect(spread_points(placed, first, second), chosen)
     b = [blocks[8 * i : 8 * i + 8] for i in range(6)]
+    copying[4].wait()
     for axis, entry in ((0, 0), (1, 3), (2, 5)):
         damp = damp_ref[axis : axis + 1, :]
         b[entry] = b[entry] + jnp.concatenate(
@@ -152,21 +170,19 @@
     inverse_ref[...] = inverse
     pulled = fetch(solve_points(inverse, sums), chosen)
     first, second = pull_points(placed, pulled, first, second)
+    copying[5].wait()
+    copying[6].wait()
+    partner_ref[0] = jnp.bitwise_xor(mask_ref[0], lax.axis_index("group"))
+    partner_ref[1] = lax.axis_index("group")
     rows = cam_ref[...] * live
-    cam_ids = cam_id_ref[...].astype(F32)
-
-    def put(ref, lo):
-        hi = lo + 128
-        ref[0:18, :] = rows[:, lo:hi]
-        ref[18:19, :] = first[:, lo:hi]
-        ref[19:20, :] = second[:, lo:hi]
-        ref[20:21, :] = cam_ids[:, lo:hi]
-        ref[21:24, :] = jnp.zeros((3, 128), F32)
-
-    for i in range(in_ref.shape[0]):
-        put(in_ref.at[i], 128 * i)
-    put(outer_ref, inner)
-    outer_sum_ref[...] = start_sums(outer_ref[...])
+    cam_ids = cam_id_ref[...].reshape(1, n).astype(F32)
+
+    every = jnp.concatenate([rows, first, second, cam_ids, jnp.zeros((3, n), F32)], 0)
+    for i in range(inner // 128):
+        in_ref[ROWS * i : ROWS * i + ROWS, :] = every[:ROWS, 128 * i : 128 * i + 128]
+    outer = every[:, inner:]
+    outer_ref[...] = outer
+    outer_sum_ref[...] = start_sums(outer)
 
 
 def spread_cams(owned, first, second):
@@ -201,7 +217,9 @@
 
 
 def blocks_of(pay_ref):
-    return jnp.concatenate([pay_ref[i] for i in range(pay_ref.shape[0])], 1)
+    rows = [pay_ref[i : i + ROWS, :] for i in range(0, pay_ref.shape[0], ROWS)]
+    owned = jnp.concatenate(rows, 1)
+    return jnp.concatenate([owned, jnp.zeros((24 - ROWS, owned.shape[1]), F32)], 0)
 
 
 def start_sum_kernel(pay_ref, outer_sum_ref, damp_ref, group_ref):
@@ -246,8 +264,11 @@
 
 
 def put_kept(back_ref, outer_sum_ref, outer_ref, kept, values):
-    inner = back_ref.shape[1]
-    put_rows(back_ref, [kept[0][:, :inner], kept[1][:, :inner], repeat(scalar_row(values), inner)])
+    inner = kept[0].shape[1] - 128
+    row = scalar_row(values)
+    for i in range(inner // 128):
+        lo, hi = 128 * i, 128 * i + 128
+        put_rows(back_ref.at[3 * i : 3 * i + 3], [kept[0][:, lo:hi], kept[1][:, lo:hi], row])
     outer = outer_ref[...]
     spread = spread_cams(outer, kept[0][:, inner:], kept[1][:, inner:])
     outer_sum_ref[...] = halves(collect(spread, ids_of(outer)))
@@ -275,15 +296,19 @@
     put_kept(back_ref, outer_sum_ref, outer_ref, kept, values)
 
 
+def back_row(back_ref, r):
+    return jnp.concatenate([back_ref[i : i + 1, :] for i in range(r, back_ref.shape[0], 3)], 1)
+
+
 def inner_image(back_ref, pay_ref, damp_ref, field):
     owned = blocks_of(pay_ref)
-    spread = spread_cams(owned, back_ref[0:1, :], back_ref[1:2, :])
+    spread = spread_cams(owned, back_row(back_ref, 0), back_row(back_ref, 1))
     return damp_ref[...] * field + halves(collect(spread, ids_of(owned)))
 
 
 def image_kernel(back_ref, outer_sum_ref, pay_ref, damp_ref, dir_ref, group_ref):
     image = inner_image(back_ref, pay_ref, damp_ref, dir_ref[0])
-    partial = lane_blocks(back_ref[2:3, :])
+    partial = lane_blocks(back_row(back_ref, 2))
     for i in range(group_ref.shape[0]):
         group_ref[i, 0:9, :] = image
         group_ref[i, 9:18, :] = outer_sum_ref[...]
@@ -316,15 +341,12 @@
     put_moved(in_ref, out_ref, pay_ref, outer_ref, scaled_ref[0], scaled_ref[1])
 
 
-def pair_kernel(back_ref, outer_sum_ref, group_ref):
-    partial = lane_blocks(back_ref[2:3, :])
+def pair_kernel(back_ref, outer_sum_ref, pay_ref, damp_ref, scaled_ref, group_ref, image_ref):
+    image_ref[...] = inner_image(back_ref, pay_ref, damp_ref, scaled_ref[0])
+    partial = lane_blocks(back_row(back_ref, 2))
     for i in range(group_ref.shape[0]):
         group_ref[i, 0:9, :] = outer_sum_ref[...]
         group_ref[i, 9:10, :] = partial
-
-
-def inner_kernel(back_ref, pay_ref, damp_ref, scaled_ref, image_ref):
-    image_ref[...] = inner_image(back_ref, pay_ref, damp_ref, scaled_ref[0])
 
 
 def last_kernel(
@@ -355,29 +377,51 @@
     )(*args)
 
 
+def start(*args):
+    n = args[0].shape[0]
+    shapes = [(ROWS * (n // 128 - 1), 128), (24, 128), (18, 128), (48, n), (48, 128), (1, n), (2,)]
+    kinds = [F32] * 5 + [jnp.int32] * 2
+    copies = [
+        pltpu.SMEM(a.shape, a.dtype) if i == 1 else pltpu.VMEM(a.shape, a.dtype)
+        for i, a in enumerate(args[:-1])
+    ]
+    args = [pltpu.with_memory_space_constraint(a, pltpu.HBM) for a in args[:-1]] + [args[-1]]
+    return pl.pallas_call(
+        setup_kernel,
+        name="setup",
+        out_shape=[jax.ShapeDtypeStruct(s, k) for s, k in zip(shapes, kinds)],
+        in_specs=[pl.BlockSpec(memory_space=pltpu.HBM)] * len(copies)
+        + [pl.BlockSpec(memory_space=pltpu.SMEM)],
+        out_specs=[pl.BlockSpec(memory_space=pltpu.VMEM)] * 6
+        + [pl.BlockSpec(memory_space=pltpu.SMEM)],
+        scratch_shapes=copies + [pltpu.SemaphoreType.DMA((len(copies),))],
+        compiler_params=pltpu.CompilerParams(vmem_limit_bytes=32 * 1024 * 1024),
+    )(*args)
+
+
 def on_device(
     cam_jac, point_jac, residuals, obs_camera, obs_point, obs_count, cam_damp, pt_damp, partner_mask
 ):
     n = cam_jac.shape[1]
     inner = n - 128
     groups = lax.axis_size("group")
-    own = lax.axis_index("group").astype(jnp.int32)
-    partner = jnp.stack([jnp.bitwise_xor(partner_mask[0], own), own])
-    point_ids = obs_point[None]
-
-    def over_dev(values, axis=1):
-        return lax.all_to_all(values, "dev", split_axis=axis, concat_axis=axis, tiled=True)
+
+    def over_dev(values):
+        return lax.all_to_all(values, "dev", split_axis=1, concat_axis=1, tiled=True)
+
+    def rows_over_dev(values):
+        blocks = values.reshape(inner // 128, -1, 1, 128)
+        got = lax.all_to_all(blocks, "dev", split_axis=0, concat_axis=0, tiled=True)
+        return got.reshape(values.shape)
 
     def over_group(values):
         return lax.all_to_all(values, "group", split_axis=0, concat_axis=0, tiled=True)
 
-    field, fields, pair, back = (9, 128), (2, 9, 128), [(2, inner), (2, 128)], (3, inner)
-    pay, outer, outer_sum, placed, inverse = call(
-        setup_kernel, "setup", 1,
-        [(inner // 128, 24, 128), (24, 128), (18, 128), (48, n), (48, 128)],
-        obs_count, cam_jac, point_jac, residuals, obs_camera[None], point_ids, pt_damp,
-    )
-    pay = over_dev(pay, 0)
+    field, fields, pair, back = (9, 128), (2, 9, 128), [(2, inner), (2, 128)], (inner // 128 * 3, 128)
+    pay, outer, outer_sum, placed, inverse, point_ids, partner = start(
+        obs_point, obs_count, point_jac, residuals, pt_damp, cam_jac, obs_camera, partner_mask
+    )
+    pay = rows_over_dev(pay)
     (sums,) = call(
         start_sum_kernel, "start_sum", 0, [(groups, 36, 128)], pay, outer_sum, cam_damp
     )
@@ -390,7 +434,7 @@
         point_first_kernel, "point_first", 0, [back, field],
         over_dev(moved), outer_moved, *points, remainder, direction,
     )
-    kept = over_dev(kept)
+    kept = rows_over_dev(kept)
     (images,) = call(
         image_kernel, "image", 0, [(groups, 19, 128)], kept, outer_sum, pay, cam_damp, direction
     )
@@ -402,9 +446,10 @@
         point_next_kernel, "point_next", 0, [back, field],
         over_dev(moved), outer_moved, *points, remainder, scaled, image,
     )
-    kept = over_dev(kept)
-    (images,) = call(pair_kernel, "pair", 0, [(groups, 10, 128)], kept, outer_sum)
-    (next_image,) = call(inner_kernel, "inner", 0, [field], kept, pay, cam_damp, scaled)
+    kept = rows_over_dev(kept)
+    images, next_image = call(
+        pair_kernel, "pair", 0, [(groups, 10, 128), field], kept, outer_sum, pay, cam_damp, scaled
+    )
     update, remainder = call(
         last_kernel, "last", 1, [field] * 2,
         partner, over_group(images), next_image, remainder, scaled, direction, image, totals,

time: 165 us -> 158 us (0.958)
  blocking collectives: 122 us -> 144 us
  waiting for transfers between devices: 14.3 us -> 0 us
  starting transfers between devices: 10.3 us -> 0 us
  local copies, waits for them, and re-layouts: 3.36 us -> 0.01 us
    all_to_all x1 -> x3, blocking collectives: 9.78 us -> 34.6 us  [over_group(): lax.all_to_all(values, 'group', split_axis=0, concat_axis=0, tiled=True)]
    all_to_all x2 -> x0, waiting for transfers between devices: 14.3 us -> none  [over_group(): lax.all_to_all(values, 'group', split_axis=0, concat_axis=0, tiled=True)]
    all_to_all x2 -> x0, starting transfers between devices: 10.3 us -> none  [over_group(): lax.all_to_all(values, 'group', split_axis=0, concat_axis=0, tiled=True)]
    pallas_call x10 -> x8, Pallas kernels: 12.3 us -> 8.39 us  [call(): pl.pallas_call(kernel, name=name, out_shape=[jax.ShapeDtypeStruct(shape,...]
    pallas_call x0 -> x1, Pallas kernels: none -> 3.76 us  [start(): pl.pallas_call(setup_kernel, name='setup', out_shape=[jax.ShapeDtypeStruc...]
    all_to_all x5, blocking collectives: 112 us -> 109 us  [the longest x3 75.1 us: rows_over_dev(): got = lax.all_to_all(blocks, 'dev', split_axis=0, concat_axis=0, tiled=True)]
    unnamed x14 -> x2, local copies, waits for them, and re-layouts: 2.6 us -> 0.01 us
  transfers between devices with their start and end apart: 2 -> 0, of which waited for: 2 -> 0; matrix products, arithmetic and copies ran while one was open for 0% -> 0% of each run, Pallas kernels for 0% -> 0%
where the time goes in v3:
time: 158 us; the launch traced here: 157 us
  blocking collectives  144 us (91%)
  Pallas kernels  12.2 us (8%)
    all_to_all x3, blocking collectives, rows_over_dev(): got = lax.all_to_all(blocks, 'dev', split_axis=0, concat_axis=0, tiled=True)  75.1 us
    all_to_all x3, blocking collectives, over_group(): lax.all_to_all(values, 'group', split_axis=0, concat_axis=0, tiled=True)  34.6 us
    all_to_all x2, blocking collectives, over_dev(): lax.all_to_all(values, 'dev', split_axis=1, concat_axis=1, tiled=True)  34.1 us
    pallas_call x8, Pallas kernels, call(): pl.pallas_call(kernel, name=name, out_shape=[jax.ShapeDtypeStruct(shape,...  8.39 us
    pallas_call x1, Pallas kernels, start(): pl.pallas_call(setup_kernel, name='setup', out_shape=[jax.ShapeDtypeStruc...  3.76 us

profile of v3, /device:TPU:1, one launch (start us, length us, event | category | flops | bytes accessed | tf_op | source)
XLA Modules:
  0.0 157.3 jit_solution(10117310101817816198)
XLA Ops:
  1.3 3.8 %setup.1 = (f32[672,128]{1,0:T(8,128)S(1)}, f32[24,128]{1,0:T(8,128)S(1)}, f32[18,128]{1,0:T(8,128)S(1)}, f32[48,4224]{1,0:T(8,128)S(1)}, f32[48,128]{1,0:T(8,12...) custom-call(s32[4224]{0:T(1024)} %refs_0_.1, s32[1,33]{1,0:T(1,128)} %refs_1_.1, f32[6,4224]{1,0:T(8,128)} %refs_2_.1, ...), custom_call_target="tpu_custom_call" | custom-call | tf_op jit(solution)/shard_map/setup/pallas_call | solution.py:389
  5.0 0.0 copy-start
  5.1 42.4 %all_to_all.52 = f32[32,21,1,128]{3,2,1,0:T(1,128)S(1)} all-to-all(f32[32,21,1,128]{3,2,1,0:T(1,128)S(1)} %bitcast.15), channel_id=1, replica_groups=mesh['group'=16,'dev'=32] {'dev'}, dimensions={0} | all-to-all | bytes 688128 | tf_op jit(solution)/shard_map/all_to_all | solution.py:414
  47.5 0.0 copy-done
  47.5 0.5 start_sum.1
  48.0 15.2 %all_to_all.53.group_ref = f32[16,36,128]{2,1,0:T(8,128)S(1)} all-to-all(f32[16,36,128]{2,1,0:T(8,128)S(1)} %start_sum.1), channel_id=1, replica_groups=mesh['group'=16,'dev'=32] {'group'}, dimensions={0} | all-to-all | bytes 589824 | tf_op jit(solution)/shard_map/all_to_all | solution.py:418
  63.2 1.2 start.1
  64.3 16.6 %all_to_all.54 = f32[2,32,128]{2,0,1:T(2,128)S(1)} all-to-all(f32[2,32,128]{2,0,1:T(2,128)S(1)} %bitcast.23), channel_id=1, replica_groups=mesh['group'=16,'dev'=32] {'dev'}, dimensions={1} | all-to-all | bytes 65536 | tf_op jit(solution)/shard_map/all_to_all | solution.py:410
  80.9 1.5 point_first.1
  82.4 16.3 %all_to_all.55 = f32[32,3,1,128]{3,2,1,0:T(1,128)S(1)} all-to-all(f32[32,3,1,128]{3,2,1,0:T(1,128)S(1)} %bitcast.21), channel_id=1, replica_groups=mesh['group'=16,'dev'=32] {'dev'}, dimensions={0} | all-to-all | bytes 98304 | tf_op jit(solution)/shard_map/all_to_all | solution.py:414
  98.8 0.5 image.1
  99.3 9.9 %all_to_all.56.group_ref = f32[16,19,128]{2,1,0:T(8,128)S(1)} all-to-all(f32[16,19,128]{2,1,0:T(8,128)S(1)} %image.1), channel_id=1, replica_groups=mesh['group'=16,'dev'=32] {'group'}, dimensions={0} | all-to-all | bytes 311296 | tf_op jit(solution)/shard_map/all_to_all | solution.py:418
  109.2 1.3 camera.1
  110.4 17.5 %all_to_all.57 = f32[2,32,128]{2,0,1:T(2,128)S(1)} all-to-all(f32[2,32,128]{2,0,1:T(2,128)S(1)} %bitcast.22), channel_id=1, replica_groups=mesh['group'=16,'dev'=32] {'dev'}, dimensions={1} | all-to-all | bytes 65536 | tf_op jit(solution)/shard_map/all_to_all | solution.py:410
  127.9 1.5 point_next.1
  129.4 16.3 %all_to_all.58 = f32[32,3,1,128]{3,2,1,0:T(1,128)S(1)} all-to-all(f32[32,3,1,128]{3,2,1,0:T(1,128)S(1)} %bitcast.20), channel_id=1, replica_groups=mesh['group'=16,'dev'=32] {'dev'}, dimensions={0} | all-to-all | bytes 98304 | tf_op jit(solution)/shard_map/all_to_all | solution.py:414
  145.8 0.5 pair.1
  146.3 9.5 %all_to_all.59.group_ref = f32[16,10,128]{2,1,0:T(8,128)S(1)} all-to-all(f32[16,10,128]{2,1,0:T(8,128)S(1)} %get-tuple-element.47), channel_id=1, replica_groups=mesh['group'=16,'dev'=32] {'group'}, dimensions={0} | all-to-all | bytes 163840 | tf_op jit(solution)/shard_map/all_to_all | solution.py:418
  155.8 1.5 last.1
Async XLA Ops:
  5.0 42.4 %copy-start = (f32[9,128]{1,0:T(8,128)S(1)}, f32[9,128]{1,0:T(8,128)}, u32[]{:S(2)}) copy-start(f32[9,128]{1,0:T(8,128)} %damp_ref.9) | copy-start | bytes 13828

commit v4 on v3

v4 whole, which is shorter than its diff:
```python
import jax
import jax.numpy as jnp
from jax import lax
from jax.experimental import pallas as pl
from jax.experimental.pallas import tpu as pltpu
from jax.sharding import PartitionSpec as P

F32 = jnp.float32
BF16 = jnp.bfloat16
STEP = 512
ROWS = 21
PAIRS = ((0, 0), (0, 1), (0, 2), (1, 1), (1, 2), (2, 2))


def one_hot(ids, count):
    rows = lax.broadcasted_iota(jnp.int32, (count, ids.shape[1]), 0)
    return jnp.where(rows == ids, 1.0, 0.0).astype(BF16)


def pieces(values, count):
    found = []
    for _ in range(count - 1):
        found.append(values.astype(BF16).astype(F32))
        values = values - found[-1]
    return jnp.concatenate(found + [values], 0).astype(BF16)


def unstack(sums, count):
    m = sums.shape[0] // count
    total = sums[0:m]
    for i in range(1, count):
        total = total + sums[i * m : (i + 1) * m]
    return total


def collect(values, chosen_t, count=2):
    return jnp.dot(pieces(values, count), chosen_t, preferred_element_type=F32)


def fetch(stacked, chosen):
    return unstack(jnp.dot(stacked, chosen, preferred_element_type=F32), 2)


def col_sum(values):
    return jnp.sum(values, axis=0, keepdims=True)


def total(values):
    return jnp.sum(values, keepdims=True)


def lane_blocks(row):
    out = row[:, 0:128]
    for b in range(1, row.shape[1] // 128):
        out = out + row[:, b * 128 : (b + 1) * 128]
    return out


def spans(n):
    return [(lo, min(lo + STEP, n)) for lo in range(0, n, STEP)]


def added(sums, more):
    return more if sums is None else sums + more


def scalar_row(values):
    lanes = lax.broadcasted_iota(jnp.int32, (1, 128), 1)
    row = jnp.broadcast_to(values[0], (1, 128))
    for i in range(1, len(values)):
        row = jnp.where(lanes < 32 * i, row, values[i])
    return row


def scalars(row, count):
    return [row[:, 32 * i : 32 * i + 1] for i in range(count)]


def put_rows(ref, rows):
    for r, row in enumerate(rows):
        ref[r : r + 1, :] = row


def solve_points(inverse, sums):
    c = [inverse[8 * i : 8 * i + 8] for i in range(6)]
    g = [sums[8 * i : 8 * i + 8] for i in range(3)]
    return jnp.concatenate(
        [
            c[0] * g[0] + c[1] * g[1] + c[2] * g[2],
            c[1] * g[0] + c[3] * g[1] + c[4] * g[2],
            c[2] * g[0] + c[4] * g[1] + c[5] * g[2],
        ],
        0,
    )


def slots_of(in_ref, out_ref, r, lo, hi):
    inner = in_ref.shape[1]
    if hi <= inner:
        return in_ref[r : r + 1, lo:hi]
    if lo >= inner:
        return out_ref[r : r + 1, lo - inner : hi - inner]
    return jnp.concatenate([in_ref[r : r + 1, lo:inner], out_ref[r : r + 1, : hi - inner]], 1)


def spread_points(placed_ref, first, second, lo, hi):
    return jnp.concatenate(
        [
            placed_ref[8 * r : 8 * r + 8, lo:hi] * first
            + placed_ref[24 + 8 * r : 32 + 8 * r, lo:hi] * second
            for r in range(3)
        ],
        0,
    )


def pull_points(placed_ref, pulled, first, second, lo, hi):
    def image(base):
        out = placed_ref[base : base + 8, lo:hi] * pulled[0:8]
        out = out + placed_ref[base + 8 : base + 16, lo:hi] * pulled[8:16]
        return col_sum(out + placed_ref[base + 16 : base + 24, lo:hi] * pulled[16:24])

    return first - image(0), second - image(24)


def setup_kernel(*refs):
    inputs, mask, outputs, copies, sems = refs[:7], refs[7], refs[8:18], refs[18:25], refs[25]
    copying = [
        pltpu.make_async_copy(source, copy, sems.at[i])
        for i, (source, copy) in enumerate(zip(inputs, copies))
    ]
    for copy in copying:
        copy.start()
    setup(copying, *copies, mask, *outputs)


def setup(
    copying, point_id_ref, count_ref, point_ref, res_ref, damp_ref, cam_ref, cam_id_ref, mask_ref,
    in_ref, outer_ref, outer_chosen_ref, outer_chosen_t_ref, outer_sum_ref, placed_ref,
    inverse_ref, chosen_ref, chosen_t_ref, partner_ref,
):
    n = cam_ref.shape[1]
    inner = n - 128
    partner = jnp.bitwise_xor(mask_ref[0], lax.axis_index("group"))
    partner_ref[...] = jnp.broadcast_to(partner, (1, 128)).astype(jnp.int32)
    copying[0].wait()
    ids = point_id_ref[...].reshape(1, n)
    low, high = jnp.bitwise_and(ids, 127), jnp.right_shift(ids, 7)
    for lo, hi in spans(n):
        chosen = one_hot(low[:, lo:hi], 128)
        chosen_ref[:, lo:hi] = chosen
        chosen_t_ref[lo:hi, :] = chosen.T
    lanes = lax.broadcasted_iota(jnp.int32, (1, 128), 1)
    copying[1].wait()
    live = jnp.concatenate(
        [jnp.where(lanes < count_ref[0, b], 1.0, 0.0) for b in range(n // 128)], 1
    )
    copying[2].wait()
    copying[3].wait()
    sums = None
    for lo, hi in spans(n):
        digit = lax.broadcasted_iota(jnp.int32, (8, hi - lo), 0)
        digit = jnp.where(digit == high[:, lo:hi], live[:, lo:hi], 0.0)
        for r in range(6):
            placed_ref[8 * r : 8 * r + 8, lo:hi] = digit * point_ref[r : r + 1, lo:hi]
        part = [placed_ref[8 * r : 8 * r + 8, lo:hi] for r in range(6)]
        terms = [part[a] * part[b] + part[3 + a] * part[3 + b] for a, b in PAIRS]
        terms.append(
            spread_points(placed_ref, res_ref[0:1, lo:hi], res_ref[1:2, lo:hi], lo, hi)
        )
        sums = added(sums, collect(jnp.concatenate(terms, 0), chosen_t_ref[lo:hi, :], 3))
    sums = unstack(sums, 3)
    b = [sums[8 * i : 8 * i + 8] for i in range(6)]
    copying[4].wait()
    for axis, entry in ((0, 0), (1, 3), (2, 5)):
        damp = damp_ref[axis : axis + 1, :]
        b[entry] = b[entry] + jnp.concatenate(
            [damp[:, 128 * h : 128 * h + 128] for h in range(8)], 0
        )
    cof = [
        b[3] * b[5] - b[4] * b[4],
        b[2] * b[4] - b[1] * b[5],
        b[1] * b[4] - b[2] * b[3],
        b[0] * b[5] - b[2] * b[2],
        b[1] * b[2] - b[0] * b[4],
        b[0] * b[3] - b[1] * b[1],
    ]
    det = b[0] * cof[0] + b[1] * cof[1] + b[2] * cof[2]
    inverse = jnp.concatenate([c / det for c in cof], 0)
    inverse_ref[...] = inverse
    stacked = pieces(solve_points(inverse, sums[48:72]), 2)
    copying[5].wait()
    copying[6].wait()
    cam_ids = cam_id_ref[...].reshape(1, n).astype(F32)
    for lo, hi in spans(n):
        pulled = fetch(stacked, chosen_ref[:, lo:hi])
        first, second = pull_points(
            placed_ref, pulled, res_ref[0:1, lo:hi], res_ref[1:2, lo:hi], lo, hi
        )
        rows = cam_ref[:, lo:hi] * live[:, lo:hi]
        every = jnp.concatenate(
            [rows, first, second, cam_ids[:, lo:hi], jnp.zeros((3, hi - lo), F32)], 0
        )
        for at in range(lo, hi, 128):
            block = every[:, at - lo : at - lo + 128]
            if at < inner:
                i = at // 128
                in_ref[ROWS * i : ROWS * i + ROWS, :] = block[:ROWS]
            else:
                outer_ref[...] = block
                outer_chosen = ids_of(block)
                outer_chosen_ref[...] = outer_chosen
                outer_chosen_t_ref[...] = outer_chosen.T
                outer_sum_ref[...] = both_halves(start_terms(block, outer_chosen.T))


def ids_of(owned):
    return one_hot(owned[20:21].astype(jnp.int32), 128)


def spread_cams(owned, first, second):
    row = lax.broadcasted_iota(jnp.int32, owned.shape, 0)
    return owned * jnp.where(row < 9, first, jnp.where(row < 18, second, 0.0))


def halves(sums):
    return sums[0:9] + sums[9:18]


def start_terms(owned, chosen_t):
    row = lax.broadcasted_iota(jnp.int32, owned.shape, 0)
    squares = jnp.where(row < 18, owned * owned, 0.0)
    terms = jnp.concatenate([spread_cams(owned, owned[18:19], owned[19:20]), squares], 0)
    return collect(terms, chosen_t)


def both_halves(sums):
    sums = unstack(sums, 2)
    return jnp.concatenate([halves(sums[0:24]), halves(sums[24:48])], 0)


def inner_of(pay_ref):
    return pay_ref.shape[0] // ROWS * 128


def owned_of(pay_ref, lo, hi):
    rows = [pay_ref[ROWS * i : ROWS * i + ROWS, :] for i in range(lo // 128, hi // 128)]
    return jnp.concatenate([jnp.concatenate(rows, 1), jnp.zeros((24 - ROWS, hi - lo), F32)], 0)


def start_sum_kernel(pay_ref, outer_sum_ref, damp_ref, group_ref, chosen_ref, chosen_t_ref):
    sums = None
    for lo, hi in spans(inner_of(pay_ref)):
        owned = owned_of(pay_ref, lo, hi)
        chosen = ids_of(owned)
        chosen_ref[:, lo:hi] = chosen
        chosen_t = chosen.T
        chosen_t_ref[lo:hi, :] = chosen_t
        sums = added(sums, start_terms(owned, chosen_t))
    sums = both_halves(sums)
    for i in range(group_ref.shape[0]):
        group_ref[i, 0:9, :] = sums[0:9]
        group_ref[i, 9:18, :] = sums[9:18] + damp_ref[...]
        group_ref[i, 18:36, :] = outer_sum_ref[...]


def twice(values):
    return pieces(jnp.concatenate([values, values, jnp.zeros((6, 128), F32)], 0), 2)


def apply_cams(owned, stacked, chosen):
    product = owned * fetch(stacked, chosen)
    row = lax.broadcasted_iota(jnp.int32, (8, owned.shape[1]), 0)
    middle = product[8:16]
    first = col_sum(product[0:8] + jnp.where(row == 0, middle, 0.0))
    second = col_sum(product[16:24] + jnp.where(row == 0, 0.0, middle))
    return first, second


def put_moved(in_ref, out_ref, pay_ref, chosen_ref, outer_ref, outer_chosen_ref, own, twin):
    stacked = twice(own)
    for lo, hi in spans(inner_of(pay_ref)):
        moved = apply_cams(owned_of(pay_ref, lo, hi), stacked, chosen_ref[:, lo:hi])
        in_ref[0:1, lo:hi], in_ref[1:2, lo:hi] = moved
    put_rows(out_ref, apply_cams(outer_ref[...], twice(twin), outer_chosen_ref[...]))


def partner_block(partner_ref, group_ref, lo, hi):
    partner = partner_ref[...]
    out = group_ref[0, lo:hi, :]
    for i in range(1, group_ref.shape[0]):
        out = jnp.where(partner == i, group_ref[i, lo:hi, :], out)
    return out


def start_kernel(
    partner_ref, group_ref, sent_ref, outer_sum_ref, pay_ref, chosen_ref, outer_ref,
    outer_chosen_ref,
    in_ref, out_ref, rem_ref, pre_ref, dir_ref,
):
    theirs = partner_block(partner_ref, group_ref, 0, 36)
    sums = [sent_ref[0, 0:18, :] + theirs[18:36], theirs[0:18] + outer_sum_ref[...]]
    for i in range(2):
        remainder = -sums[i][0:9]
        precond = 1.0 / sums[i][9:18]
        rem_ref[i] = remainder
        pre_ref[i] = precond
        dir_ref[i] = precond * remainder
    put_moved(
        in_ref, out_ref, pay_ref, chosen_ref, outer_ref, outer_chosen_ref, dir_ref[0], dir_ref[1]
    )


def point_side(
    in_ref, out_ref, placed_ref, chosen_ref, chosen_t_ref, inverse_ref, outer_ref,
    outer_chosen_t_ref, back_ref, outer_sum_ref, values,
):
    n = placed_ref.shape[1]
    inner = n - 128
    sums = None
    for lo, hi in spans(n):
        first, second = slots_of(in_ref, out_ref, 0, lo, hi), slots_of(in_ref, out_ref, 1, lo, hi)
        terms = spread_points(placed_ref, first, second, lo, hi)
        sums = added(sums, collect(terms, chosen_t_ref[lo:hi, :]))
    stacked = pieces(solve_points(inverse_ref[...], unstack(sums, 2)), 2)
    bend = None
    for lo, hi in spans(n):
        first, second = slots_of(in_ref, out_ref, 0, lo, hi), slots_of(in_ref, out_ref, 1, lo, hi)
        pulled = fetch(stacked, chosen_ref[:, lo:hi])
        kept = pull_points(placed_ref, pulled, first, second, lo, hi)
        bend = added(bend, lane_blocks(first * kept[0] + second * kept[1]))
        for at in range(lo, hi, 128):
            rows = [k[:, at - lo : at - lo + 128] for k in kept]
            if at < inner:
                i = 3 * (at // 128)
                back_ref[i : i + 1, :], back_ref[i + 1 : i + 2, :] = rows
            else:
                spread = spread_cams(outer_ref[...], *rows)
                outer = collect(spread, outer_chosen_t_ref[...])
                outer_sum_ref[...] = halves(unstack(outer, 2))
    values[1] = values[1] + total(bend)
    row = scalar_row(values)
    for i in range(inner // 128):
        back_ref[3 * i + 2 : 3 * i + 3, :] = row


def point_first_kernel(
    in_ref, out_ref, placed_ref, chosen_ref, chosen_t_ref, inverse_ref, outer_ref,
    outer_chosen_t_ref, damp_ref,
    rem_ref, dir_ref,
    back_ref, outer_sum_ref,
):
    direction = dir_ref[0]
    values = [total(rem_ref[0] * direction), total(damp_ref[...] * direction * direction)]
    point_side(
        in_ref, out_ref, placed_ref, chosen_ref, chosen_t_ref, inverse_ref, outer_ref,
        outer_chosen_t_ref, back_ref, outer_sum_ref, values,
    )


def point_next_kernel(
    in_ref, out_ref, placed_ref, chosen_ref, chosen_t_ref, inverse_ref, outer_ref,
    outer_chosen_t_ref, damp_ref,
    rem_ref, scaled_ref, image_ref,
    back_ref, outer_sum_ref,
):
    scaled = scaled_ref[0]
    values = [
        total(rem_ref[0] * scaled),
        total(damp_ref[...] * scaled * scaled),
        total(image_ref[...] * scaled),
    ]
    point_side(
        in_ref, out_ref, placed_ref, chosen_ref, chosen_t_ref, inverse_ref, outer_ref,
        outer_chosen_t_ref, back_ref, outer_sum_ref, values,
    )


def back_row(back_ref, r, lo, hi):
    rows = [back_ref[3 * i + r : 3 * i + r + 1, :] for i in range(lo // 128, hi // 128)]
    return jnp.concatenate(rows, 1)


def inner_image(back_ref, pay_ref, chosen_t_ref, damp_ref, field):
    sums = None
    row = None
    for lo, hi in spans(inner_of(pay_ref)):
        first, second = back_row(back_ref, 0, lo, hi), back_row(back_ref, 1, lo, hi)
        spread = spread_cams(owned_of(pay_ref, lo, hi), first, second)
        sums = added(sums, collect(spread, chosen_t_ref[lo:hi, :]))
        row = added(row, lane_blocks(back_row(back_ref, 2, lo, hi)))
    return damp_ref[...] * field + halves(unstack(sums, 2)), row


def image_kernel(back_ref, outer_sum_ref, pay_ref, chosen_t_ref, damp_ref, dir_ref, group_ref):
    image, partial = inner_image(back_ref, pay_ref, chosen_t_ref, damp_ref, dir_ref[0])
    for i in range(group_ref.shape[0]):
        group_ref[i, 0:9, :] = image
        group_ref[i, 9:18, :] = outer_sum_ref[...]
        group_ref[i, 18:19, :] = partial


def group_total(group_ref, r):
    row = group_ref[0, r : r + 1, :]
    for i in range(1, group_ref.shape[0]):
        row = row + group_ref[i, r : r + 1, :]
    return row


def camera_kernel(
    partner_ref, group_ref, sent_ref, outer_sum_ref, pay_ref, chosen_ref, outer_ref,
    outer_chosen_ref, rem_ref, pre_ref, dir_ref,
    in_ref, out_ref, next_rem_ref, scaled_ref, image_ref, sums_ref,
):
    sums = group_total(group_ref, 18)
    sums_ref[...] = sums
    norm, bend = scalars(sums, 2)
    step = norm / bend
    theirs = partner_block(partner_ref, group_ref, 0, 18)
    images = [sent_ref[0, 0:9, :] + theirs[9:18], theirs[0:9] + outer_sum_ref[...]]
    image_ref[...] = images[0]
    for i in range(2):
        remainder = rem_ref[i] - step * images[i]
        next_rem_ref[i] = remainder
        scaled_ref[i] = pre_ref[i] * remainder
    put_moved(
        in_ref, out_ref, pay_ref, chosen_ref, outer_ref, outer_chosen_ref,
        scaled_ref[0], scaled_ref[1],
    )


def pair_kernel(
    back_ref, outer_sum_ref, pay_ref, chosen_t_ref, damp_ref, scaled_ref, group_ref, image_ref
):
    image, partial = inner_image(back_ref, pay_ref, chosen_t_ref, damp_ref, scaled_ref[0])
    image_ref[...] = image
    for i in range(group_ref.shape[0]):
        group_ref[i, 0:9, :] = outer_sum_ref[...]
        group_ref[i, 9:10, :] = partial


def last_kernel(
    partner_ref, group_ref, inner_ref, rem_ref, scaled_ref, dir_ref, image_ref, sums_ref,
    update_ref, next_rem_ref,
):
    norm, bend = scalars(sums_ref[...], 2)
    next_norm, next_bend, cross = scalars(group_total(group_ref, 9), 3)
    ratio = next_norm / norm
    next_bend = next_bend + ratio * (2.0 * cross + ratio * bend)
    step = next_norm / next_bend
    theirs = partner_block(partner_ref, group_ref, 0, 9)
    image = inner_ref[...] + theirs + ratio * image_ref[...]
    direction = dir_ref[0]
    update_ref[...] = norm / bend * direction + step * (scaled_ref[0] + ratio * direction)
    next_rem_ref[...] = rem_ref[0] - step * image


def call(kernel, name, shapes, *args):
    vmem = pl.BlockSpec(memory_space=pltpu.VMEM)
    return pl.pallas_call(
        kernel,
        name=name,
        out_shape=[jax.ShapeDtypeStruct(*shape) for shape in shapes],
        in_specs=[vmem] * len(args),
        out_specs=[vmem] * len(shapes),
        compiler_params=pltpu.CompilerParams(vmem_limit_bytes=32 * 1024 * 1024),
    )(*args)


def start(*args):
    n = args[0].shape[0]
    shapes = [
        ((ROWS * (n // 128 - 1), 128), F32),
        ((24, 128), F32),
        ((128, 128), BF16),
        ((128, 128), BF16),
        ((18, 128), F32),
        ((48, n), F32),
        ((48, 128), F32),
        ((128, n), BF16),
        ((n, 128), BF16),
        ((1, 128), jnp.int32),
    ]
    copies = [
        pltpu.SMEM(a.shape, a.dtype) if i == 1 else pltpu.VMEM(a.shape, a.dtype)
        for i, a in enumerate(args[:-1])
    ]
    args = [pltpu.with_memory_space_constraint(a, pltpu.HBM) for a in args[:-1]] + [args[-1]]
    return pl.pallas_call(
        setup_kernel,
        name="setup",
        out_shape=[jax.ShapeDtypeStruct(*shape) for shape in shapes],
        in_specs=[pl.BlockSpec(memory_space=pltpu.HBM)] * len(copies)
        + [pl.BlockSpec(memory_space=pltpu.SMEM)],
        out_specs=[pl.BlockSpec(memory_space=pltpu.VMEM)] * len(shapes),
        scratch_shapes=copies + [pltpu.SemaphoreType.DMA((len(copies),))],
        compiler_params=pltpu.CompilerParams(vmem_limit_bytes=32 * 1024 * 1024),
    )(*args)


def on_device(
    cam_jac, point_jac, residuals, obs_camera, obs_point, obs_count, cam_damp, pt_damp, partner_mask
):
    n = cam_jac.shape[1]
    inner = n - 128
    groups = lax.axis_size("group")

    def over_dev(values):
        return lax.all_to_all(values, "dev", split_axis=1, concat_axis=1, tiled=True)

    def rows_over_dev(values):
        blocks = values.reshape(inner // 128, -1, 1, 128)
        got = lax.all_to_all(blocks, "dev", split_axis=0, concat_axis=0, tiled=True)
        return got.reshape(values.shape)

    def over_group(values):
        return lax.all_to_all(values, "group", split_axis=0, concat_axis=0, tiled=True)

    def sends(rows):
        return ((groups, rows, 128), F32)

    field, fields, line = ((9, 128), F32), ((2, 9, 128), F32), ((1, 128), F32)
    pair, back = [((2, inner), F32), ((2, 128), F32)], ((inner // 128 * 3, 128), F32)
    pay, outer, outer_chosen, outer_chosen_t, outer_sum, placed, inverse, *ones, partner = start(
        obs_point, obs_count, point_jac, residuals, pt_damp, cam_jac, obs_camera, partner_mask
    )
    pay = rows_over_dev(pay)
    sums, chosen, chosen_t = call(
        start_sum_kernel, "start_sum", [sends(36), ((128, inner), BF16), ((inner, 128), BF16)],
        pay, outer_sum, cam_damp,
    )
    cameras = (pay, chosen, outer, outer_chosen)
    moved, outer_moved, remainder, precond, direction = call(
        start_kernel, "start", pair + [fields] * 3,
        partner, over_group(sums), sums, outer_sum, *cameras,
    )
    points = (placed, *ones, inverse, outer, outer_chosen_t, cam_damp)
    kept, outer_sum = call(
        point_first_kernel, "point_first", [back, field],
        over_dev(moved), outer_moved, *points, remainder, direction,
    )
    kept = rows_over_dev(kept)
    (images,) = call(
        image_kernel, "image", [sends(19)], kept, outer_sum, pay, chosen_t, cam_damp, direction
    )
    moved, outer_moved, remainder, scaled, image, totals = call(
        camera_kernel, "camera", pair + [fields] * 2 + [field, line],
        partner, over_group(images), images, outer_sum, *cameras, remainder, precond, direction,
    )
    kept, outer_sum = call(
        point_next_kernel, "point_next", [back, field],
        over_dev(moved), outer_moved, *points, remainder, scaled, image,
    )
    kept = rows_over_dev(kept)
    images, next_image = call(
        pair_kernel, "pair", [sends(10), field], kept, outer_sum, pay, chosen_t, cam_damp, scaled
    )
    update, remainder = call(
        last_kernel, "last", [field] * 2,
        partner, over_group(images), next_image, remainder, scaled, direction, image, totals,
    )
    return (update, remainder)


def solution(mesh):
    slots, rows = P(None, ("group", "dev")), P(("group", "dev"))
    return jax.shard_map(
        on_device,
        mesh=mesh,
        in_specs=(
            slots, slots, slots, rows, rows, P(("group", "dev"), None), slots, slots, P("dev"),
        ),
        out_specs=(slots, slots),
        check_vma=False,
    )
```

time: 158 us -> 153 us (0.968)
  Pallas kernels: 12.2 us -> 7.22 us
    pallas_call x8, Pallas kernels: 8.39 us -> 4.67 us  [call(): pl.pallas_call(kernel, name=name, out_shape=[jax.ShapeDtypeStruct(*shape)...]
where the time goes in v4:
time: 153 us; the launch traced here: 152 us
  blocking collectives  144 us (94%)
  Pallas kernels  7.22 us (5%)
    all_to_all x3, blocking collectives, rows_over_dev(): got = lax.all_to_all(blocks, 'dev', split_axis=0, concat_axis=0, tiled=True)  75.1 us
    all_to_all x3, blocking collectives, over_group(): lax.all_to_all(values, 'group', split_axis=0, concat_axis=0, tiled=True)  34.6 us
    all_to_all x2, blocking collectives, over_dev(): lax.all_to_all(values, 'dev', split_axis=1, concat_axis=1, tiled=True)  34.1 us
    pallas_call x8, Pallas kernels, call(): pl.pallas_call(kernel, name=name, out_shape=[jax.ShapeDtypeStruct(*shape)...  4.67 us

profile of v4, /device:TPU:1, one launch (start us, length us, event | category | flops | bytes accessed | tf_op | source)
XLA Modules:
  0.0 152.4 jit_solution(2795230882839176396)
XLA Ops:
  0.6 0.0 copy-start
  1.3 2.5 %setup.1 = (f32[672,128]{1,0:T(8,128)S(1)}, f32[24,128]{1,0:T(8,128)S(1)}, bf16[128,128]{1,0:T(8,128)(2,1)S(1)}, bf16[128,128]{1,0:T(8,128)(2,1)S(1)}, f32[18,12...) custom-call(s32[4224]{0:T(1024)} %refs_0_.1, ...), custom_call_target="tpu_custom_call" | custom-call | tf_op jit(solution)/shard_map/setup/pallas_call | solution.py:489
  3.9 42.4 %all_to_all.52 = f32[32,21,1,128]{3,2,1,0:T(1,128)S(1)} all-to-all(f32[32,21,1,128]{3,2,1,0:T(1,128)S(1)} %bitcast.15), channel_id=1, replica_groups=mesh['group'=16,'dev'=32] {'dev'}, dimensions={0} | all-to-all | bytes 688128 | tf_op jit(solution)/shard_map/all_to_all | solution.py:513
  46.3 0.0 copy-done
  46.3 0.7 start_sum.1
  47.0 15.2 %all_to_all.53.group_ref = f32[16,36,128]{2,1,0:T(8,128)S(1)} all-to-all(f32[16,36,128]{2,1,0:T(8,128)S(1)} %get-tuple-element.35.sent_ref), channel_id=1, replica_groups=mesh['group'=16,'dev'=32] {'group'}, dimensions={0} | all-to-all | bytes 589824 | tf_op jit(solution)/shard_map/all_to_all | solution.py:517
  62.2 0.3 start.1
  62.6 16.6 %all_to_all.54 = f32[2,32,128]{2,0,1:T(2,128)S(1)} all-to-all(f32[2,32,128]{2,0,1:T(2,128)S(1)} %bitcast.23), channel_id=1, replica_groups=mesh['group'=16,'dev'=32] {'dev'}, dimensions={1} | all-to-all | bytes 65536 | tf_op jit(solution)/shard_map/all_to_all | solution.py:509
  79.1 0.8 point_first.1
  79.9 16.3 %all_to_all.55 = f32[32,3,1,128]{3,2,1,0:T(1,128)S(1)} all-to-all(f32[32,3,1,128]{3,2,1,0:T(1,128)S(1)} %bitcast.21), channel_id=1, replica_groups=mesh['group'=16,'dev'=32] {'dev'}, dimensions={0} | all-to-all | bytes 98304 | tf_op jit(solution)/shard_map/all_to_all | solution.py:513
  96.3 0.3 image.1.sent_ref
  96.6 9.9 %all_to_all.56.group_ref = f32[16,19,128]{2,1,0:T(8,128)S(1)} all-to-all(f32[16,19,128]{2,1,0:T(8,128)S(1)} %image.1.sent_ref), channel_id=1, replica_groups=mesh['group'=16,'dev'=32] {'group'}, dimensions={0} | all-to-all | bytes 311296 | tf_op jit(solution)/shard_map/all_to_all | solution.py:517
  106.5 0.4 camera.1
  106.9 17.5 %all_to_all.57 = f32[2,32,128]{2,0,1:T(2,128)S(1)} all-to-all(f32[2,32,128]{2,0,1:T(2,128)S(1)} %bitcast.22), channel_id=1, replica_groups=mesh['group'=16,'dev'=32] {'dev'}, dimensions={1} | all-to-all | bytes 65536 | tf_op jit(solution)/shard_map/all_to_all | solution.py:509
  124.4 0.8 point_next.1
  125.2 16.3 %all_to_all.58 = f32[32,3,1,128]{3,2,1,0:T(1,128)S(1)} all-to-all(f32[32,3,1,128]{3,2,1,0:T(1,128)S(1)} %bitcast.20), channel_id=1, replica_groups=mesh['group'=16,'dev'=32] {'dev'}, dimensions={0} | all-to-all | bytes 98304 | tf_op jit(solution)/shard_map/all_to_all | solution.py:513
  141.6 0.3 pair.1
  141.9 9.5 %all_to_all.59.group_ref = f32[16,10,128]{2,1,0:T(8,128)S(1)} all-to-all(f32[16,10,128]{2,1,0:T(8,128)S(1)} %get-tuple-element.59), channel_id=1, replica_groups=mesh['group'=16,'dev'=32] {'group'}, dimensions={0} | all-to-all | bytes 163840 | tf_op jit(solution)/shard_map/all_to_all | solution.py:517
  151.4 1.0 last.1
Async XLA Ops:
  0.6 45.6 %copy-start = (f32[9,128]{1,0:T(8,128)S(1)}, f32[9,128]{1,0:T(8,128)}, u32[]{:S(2)}) copy-start(f32[9,128]{1,0:T(8,128)} %damp_ref.9) | copy-start | bytes 13828

commit v5 on v4

--- a/solution.py
+++ b/solution.py
@@ -124,7 +124,7 @@
 
 
 def setup_kernel(*refs):
-    inputs, mask, outputs, copies, sems = refs[:7], refs[7], refs[8:18], refs[18:25], refs[25]
+    inputs, mask, outputs, copies, sems = refs[:8], refs[8], refs[9:21], refs[21:29], refs[29]
     copying = [
         pltpu.make_async_copy(source, copy, sems.at[i])
         for i, (source, copy) in enumerate(zip(inputs, copies))
@@ -135,8 +135,9 @@
 
 
 def setup(
-    copying, point_id_ref, count_ref, point_ref, res_ref, damp_ref, cam_ref, cam_id_ref, mask_ref,
-    in_ref, outer_ref, outer_chosen_ref, outer_chosen_t_ref, outer_sum_ref, placed_ref,
+    copying, point_id_ref, count_ref, point_ref, res_ref, damp_ref, cam_ref, cam_id_ref,
+    cam_damp_ref, mask_ref,
+    same_ref, cross_ref, damp_out_ref, outer_ref, outer_chosen_ref, outer_chosen_t_ref, outer_sum_ref, placed_ref,
     inverse_ref, chosen_ref, chosen_t_ref, partner_ref,
 ):
     n = cam_ref.shape[1]
@@ -191,7 +192,10 @@
     stacked = pieces(solve_points(inverse, sums[48:72]), 2)
     copying[5].wait()
     copying[6].wait()
+    copying[7].wait()
+    damp_out_ref[...] = cam_damp_ref[...]
     cam_ids = cam_id_ref[...].reshape(1, n).astype(F32)
+    core = jnp.bitwise_and(lax.axis_index("dev"), 1)
     for lo, hi in spans(n):
         pulled = fetch(stacked, chosen_ref[:, lo:hi])
         first, second = pull_points(
@@ -201,17 +205,19 @@
         every = jnp.concatenate(
             [rows, first, second, cam_ids[:, lo:hi], jnp.zeros((3, hi - lo), F32)], 0
         )
-        for at in range(lo, hi, 128):
-            block = every[:, at - lo : at - lo + 128]
-            if at < inner:
-                i = at // 128
-                in_ref[ROWS * i : ROWS * i + ROWS, :] = block[:ROWS]
-            else:
-                outer_ref[...] = block
-                outer_chosen = ids_of(block)
-                outer_chosen_ref[...] = outer_chosen
-                outer_chosen_t_ref[...] = outer_chosen.T
-                outer_sum_ref[...] = both_halves(start_terms(block, outer_chosen.T))
+        for at in range(lo, min(hi, inner), 256):
+            even = every[:ROWS, at - lo : at - lo + 128]
+            odd = every[:ROWS, at - lo + 128 : at - lo + 256]
+            i = ROWS * (at // 256)
+            same_ref[i : i + ROWS, :] = jnp.where(core == 0, even, odd)
+            cross_ref[i : i + ROWS, :] = jnp.where(core == 0, odd, even)
+        if hi > inner:
+            block = every[:, inner - lo :]
+            outer_ref[...] = block
+            outer_chosen = ids_of(block)
+            outer_chosen_ref[...] = outer_chosen
+            outer_chosen_t_ref[...] = outer_chosen.T
+            outer_sum_ref[...] = both_halves(start_terms(block, outer_chosen.T))
 
 
 def ids_of(owned):
@@ -248,9 +254,23 @@
     return jnp.concatenate([jnp.concatenate(rows, 1), jnp.zeros((24 - ROWS, hi - lo), F32)], 0)
 
 
-def start_sum_kernel(pay_ref, outer_sum_ref, damp_ref, group_ref, chosen_ref, chosen_t_ref):
+def merge_kernel(same_ref, crossed_ref, both_ref):
+    for i in range(0, same_ref.shape[0], ROWS):
+        both_ref[2 * i : 2 * i + ROWS, :] = same_ref[i : i + ROWS, :]
+        both_ref[2 * i + ROWS : 2 * i + 2 * ROWS, :] = crossed_ref[i : i + ROWS, :]
+
+
+def start_sum_kernel(
+    got_ref, outer_sum_ref, damp_ref, group_ref, chosen_ref, chosen_t_ref, pay_ref
+):
+    core = jnp.bitwise_and(lax.axis_index("dev"), 1)
     sums = None
     for lo, hi in spans(inner_of(pay_ref)):
+        for i in range(ROWS * (lo // 128), ROWS * (hi // 128), 2 * ROWS):
+            first = got_ref[i : i + ROWS, :]
+            second = got_ref[i + ROWS : i + 2 * ROWS, :]
+            pay_ref[i : i + ROWS, :] = jnp.where(core == 0, first, second)
+            pay_ref[i + ROWS : i + 2 * ROWS, :] = jnp.where(core == 0, second, first)
         owned = owned_of(pay_ref, lo, hi)
         chosen = ids_of(owned)
         chosen_ref[:, lo:hi] = chosen
@@ -470,7 +490,9 @@
 def start(*args):
     n = args[0].shape[0]
     shapes = [
-        ((ROWS * (n // 128 - 1), 128), F32),
+        ((ROWS * (n // 256), 128), F32),
+        ((ROWS * (n // 256), 128), F32),
+        ((9, 128), F32),
         ((24, 128), F32),
         ((128, 128), BF16),
         ((128, 128), BF16),
@@ -513,6 +535,16 @@
         got = lax.all_to_all(blocks, "dev", split_axis=0, concat_axis=0, tiled=True)
         return got.reshape(values.shape)
 
+    def over_chips(same, cross):
+        count = lax.axis_size("dev")
+        crossed = lax.ppermute(cross, "dev", [(i, i ^ 1) for i in range(count)])
+        (both,) = call(merge_kernel, "merge", [((ROWS * count, 128), F32)], same, crossed)
+        got = lax.all_to_all(
+            both.reshape(count // 2, 2 * ROWS, 1, 128), "dev", split_axis=0, concat_axis=0, tiled=True,
+            axis_index_groups=[list(range(c, count, 2)) for c in range(2)],
+        )
+        return got.reshape(-1, 128)
+
     def over_group(values):
         return lax.all_to_all(values, "group", split_axis=0, concat_axis=0, tiled=True)
 
@@ -521,12 +553,17 @@
 
     field, fields, line = ((9, 128), F32), ((2, 9, 128), F32), ((1, 128), F32)
     pair, back = [((2, inner), F32), ((2, 128), F32)], ((inner // 128 * 3, 128), F32)
-    pay, outer, outer_chosen, outer_chosen_t, outer_sum, placed, inverse, *ones, partner = start(
-        obs_point, obs_count, point_jac, residuals, pt_damp, cam_jac, obs_camera, partner_mask
-    )
-    pay = rows_over_dev(pay)
-    sums, chosen, chosen_t = call(
-        start_sum_kernel, "start_sum", [sends(36), ((128, inner), BF16), ((inner, 128), BF16)],
+    (
+        same, cross, cam_damp, outer, outer_chosen, outer_chosen_t, outer_sum, placed, inverse,
+        *ones, partner,
+    ) = start(
+        obs_point, obs_count, point_jac, residuals, pt_damp, cam_jac, obs_camera, cam_damp,
+        partner_mask,
+    )
+    pay = over_chips(same, cross)
+    sums, chosen, chosen_t, pay = call(
+        start_sum_kernel, "start_sum",
+        [sends(36), ((128, inner), BF16), ((inner, 128), BF16), (pay.shape, F32)],
         pay, outer_sum, cam_damp,
     )
     cameras = (pay, chosen, outer, outer_chosen)

time: 153 us -> 155 us (1.013)
  starting transfers between devices: 0 us -> 8.78 us
  blocking collectives: 144 us -> 136 us
    all_to_all x3 -> x2, blocking collectives: 75.1 us -> 32.8 us  [rows_over_dev(): got = lax.all_to_all(blocks, 'dev', split_axis=0, concat_axis=0, tiled=True)]
    all_to_all x0 -> x1, blocking collectives: none -> 25.1 us  [over_chips(): lax.all_to_all(both.reshape(count // 2, 2 * ROWS, 1, 128), 'dev', split_a...]
    all_to_all x2, blocking collectives: 34.1 us -> 44.3 us  [over_dev(): lax.all_to_all(values, 'dev', split_axis=1, concat_axis=1, tiled=True)]
    ppermute x0 -> x1, starting transfers between devices: none -> 8.78 us  [over_chips(): crossed = lax.ppermute(cross, 'dev', [(i, i ^ 1) for i in range(count)])]
    pallas_call x8 -> x9, Pallas kernels: 4.67 us -> 4.73 us  [call(): pl.pallas_call(kernel, name=name, out_shape=[jax.ShapeDtypeStruct(*shape)...]
  transfers between devices with their start and end apart: 0 -> 1, of which waited for: 0 -> 1; matrix products, arithmetic and copies ran while one was open for 0% -> 0% of each run, Pallas kernels for 0% -> 0%
where the time goes in v5:
time: 155 us; the launch traced here: 154 us
  blocking collectives  136 us (88%)
  starting transfers between devices  8.78 us (6%)
  Pallas kernels  7.3 us (5%)
    all_to_all x2, blocking collectives, over_dev(): lax.all_to_all(values, 'dev', split_axis=1, concat_axis=1, tiled=True)  44.3 us
    all_to_all x3, blocking collectives, over_group(): lax.all_to_all(values, 'group', split_axis=0, concat_axis=0, tiled=True)  33.9 us
    all_to_all x2, blocking collectives, rows_over_dev(): got = lax.all_to_all(blocks, 'dev', split_axis=0, concat_axis=0, tiled=True)  32.8 us
    all_to_all x1, blocking collectives, over_chips(): lax.all_to_all(both.reshape(count // 2, 2 * ROWS, 1, 128), 'dev', split_a...  25.1 us
    ppermute x1, starting transfers between devices, over_chips(): crossed = lax.ppermute(cross, 'dev', [(i, i ^ 1) for i in range(count)])  8.78 us
    pallas_call x9, Pallas kernels, call(): pl.pallas_call(kernel, name=name, out_shape=[jax.ShapeDtypeStruct(*shape)...  4.73 us
  transfers between devices with their start and end apart: 1, of which 1 were waited for; matrix products, arithmetic and copies ran while one was open for 0% of the time, Pallas kernels for 0%

profile of v5, /device:TPU:1, one launch (start us, length us, event | category | flops | bytes accessed | tf_op | source)
XLA Modules:
  0.0 154.5 jit_solution(12210851406935631841)
XLA Ops:
  1.3 2.6 %setup.1 = (f32[336,128]{1,0:T(8,128)S(1)}, f32[336,128]{1,0:T(8,128)S(1)}, f32[9,128]{1,0:T(8,128)S(1)}, f32[24,128]{1,0:T(8,128)S(1)}, bf16[128,128]{1,0:T(8,1...) custom-call(s32[4224]{0:T(1024)} %refs_0_.1, ...), custom_call_target="tpu_custom_call" | custom-call | tf_op jit(solution)/shard_map/setup/pallas_call | solution.py:511
  3.9 8.8 %collective-permute-start = (f32[336,128]{1,0:T(8,128)S(1)}, f32[336,128]{1,0:T(8,128)S(1)}, u32[]{:S(2)}, u32[]{:S(2)}) collective-permute-start(f32[336,128]{1,0:T(8,128)S(1)} %get-tuple-element.37), channel_id=1, source_target_pairs={{0,1},{1,0},{2,3},{3,2},{4,5},{5,4},{6,7},{7,6},{8,9},{9,8},{10,11... | collective-permute-start | bytes 516104 | tf_op jit(solution)/shard_map/ppermute | solution.py:540
  12.7 1.0 collective-permute-done.crossed_ref
  13.7 25.1 %all_to_all.52 = f32[16,42,1,128]{3,2,1,0:T(1,128)S(1)} all-to-all(f32[16,42,1,128]{3,2,1,0:T(1,128)S(1)} %bitcast.11), channel_id=1, replica_groups={{0,2,4,6,8,10,12,14,16,18,20,22,24,26,28,30},{1,3,5,7,9,11,13,15,17,19,..., dimensions={0} | all-to-all | bytes 688128 | tf_op jit(solution)/shard_map/all_to_all | solution.py:542
  38.8 0.8 start_sum.1
  39.5 14.5 %all_to_all.53.group_ref = f32[16,36,128]{2,1,0:T(8,128)S(1)} all-to-all(f32[16,36,128]{2,1,0:T(8,128)S(1)} %get-tuple-element.40.sent_ref), channel_id=1, replica_groups=mesh['group'=16,'dev'=32] {'group'}, dimensions={0} | all-to-all | bytes 589824 | tf_op jit(solution)/shard_map/all_to_all | solution.py:549
  54.0 0.3 start.1
  54.3 26.7 %all_to_all.54 = f32[2,32,128]{2,0,1:T(2,128)S(1)} all-to-all(f32[2,32,128]{2,0,1:T(2,128)S(1)} %bitcast.19), channel_id=1, replica_groups=mesh['group'=16,'dev'=32] {'dev'}, dimensions={1} | all-to-all | bytes 65536 | tf_op jit(solution)/shard_map/all_to_all | solution.py:531
  81.1 0.8 point_first.1
  81.8 16.4 %all_to_all.55 = f32[32,3,1,128]{3,2,1,0:T(1,128)S(1)} all-to-all(f32[32,3,1,128]{3,2,1,0:T(1,128)S(1)} %bitcast.17), channel_id=1, replica_groups=mesh['group'=16,'dev'=32] {'dev'}, dimensions={0} | all-to-all | bytes 98304 | tf_op jit(solution)/shard_map/all_to_all | solution.py:535
  98.3 0.3 image.1.sent_ref
  98.6 9.9 %all_to_all.56.group_ref = f32[16,19,128]{2,1,0:T(8,128)S(1)} all-to-all(f32[16,19,128]{2,1,0:T(8,128)S(1)} %image.1.sent_ref), channel_id=1, replica_groups=mesh['group'=16,'dev'=32] {'group'}, dimensions={0} | all-to-all | bytes 311296 | tf_op jit(solution)/shard_map/all_to_all | solution.py:549
  108.5 0.4 camera.1
  108.9 17.5 %all_to_all.57 = f32[2,32,128]{2,0,1:T(2,128)S(1)} all-to-all(f32[2,32,128]{2,0,1:T(2,128)S(1)} %bitcast.18), channel_id=1, replica_groups=mesh['group'=16,'dev'=32] {'dev'}, dimensions={1} | all-to-all | bytes 65536 | tf_op jit(solution)/shard_map/all_to_all | solution.py:531
  126.5 0.8 point_next.1
  127.3 16.3 %all_to_all.58 = f32[32,3,1,128]{3,2,1,0:T(1,128)S(1)} all-to-all(f32[32,3,1,128]{3,2,1,0:T(1,128)S(1)} %bitcast.16), channel_id=1, replica_groups=mesh['group'=16,'dev'=32] {'dev'}, dimensions={0} | all-to-all | bytes 98304 | tf_op jit(solution)/shard_map/all_to_all | solution.py:535
  143.6 0.3 pair.1
  143.9 9.5 %all_to_all.59.group_ref = f32[16,10,128]{2,1,0:T(8,128)S(1)} all-to-all(f32[16,10,128]{2,1,0:T(8,128)S(1)} %get-tuple-element.65), channel_id=1, replica_groups=mesh['group'=16,'dev'=32] {'group'}, dimensions={0} | all-to-all | bytes 163840 | tf_op jit(solution)/shard_map/all_to_all | solution.py:549
  153.5 1.0 last.1
  (1 shorter events, 0.0 us)
Async XLA Ops:
  3.9 9.8 %collective-permute-start = (f32[336,128]{1,0:T(8,128)S(1)}, f32[336,128]{1,0:T(8,128)S(1)}, u32[]{:S(2)}, u32[]{:S(2)}) collective-permute-start(f32[336,128]{1,0:T(8,128)S(1)} %get-tuple-element.37), channel_id=1, source_target_pairs={{0,1},{1,0},{2,3},{3,2},{4,5},{5,4},{6,7},{7,6},{8,9},{9,8},{10,11... | collective-permute-start | bytes 516104 | tf_op jit(solution)/shard_map/ppermute | solution.py:540

commit v6 on v4

--- a/solution.py
+++ b/solution.py
@@ -124,7 +124,7 @@
 
 
 def setup_kernel(*refs):
-    inputs, mask, outputs, copies, sems = refs[:7], refs[7], refs[8:18], refs[18:25], refs[25]
+    inputs, mask, outputs, copies, sems = refs[:8], refs[8], refs[9:20], refs[20:28], refs[28]
     copying = [
         pltpu.make_async_copy(source, copy, sems.at[i])
         for i, (source, copy) in enumerate(zip(inputs, copies))
@@ -135,8 +135,9 @@
 
 
 def setup(
-    copying, point_id_ref, count_ref, point_ref, res_ref, damp_ref, cam_ref, cam_id_ref, mask_ref,
-    in_ref, outer_ref, outer_chosen_ref, outer_chosen_t_ref, outer_sum_ref, placed_ref,
+    copying, point_id_ref, count_ref, point_ref, res_ref, damp_ref, cam_ref, cam_id_ref,
+    cam_damp_ref, mask_ref,
+    in_ref, damp_out_ref, outer_ref, outer_chosen_ref, outer_chosen_t_ref, outer_sum_ref, placed_ref,
     inverse_ref, chosen_ref, chosen_t_ref, partner_ref,
 ):
     n = cam_ref.shape[1]
@@ -191,6 +192,8 @@
     stacked = pieces(solve_points(inverse, sums[48:72]), 2)
     copying[5].wait()
     copying[6].wait()
+    copying[7].wait()
+    damp_out_ref[...] = cam_damp_ref[...]
     cam_ids = cam_id_ref[...].reshape(1, n).astype(F32)
     for lo, hi in spans(n):
         pulled = fetch(stacked, chosen_ref[:, lo:hi])
@@ -471,6 +474,7 @@
     n = args[0].shape[0]
     shapes = [
         ((ROWS * (n // 128 - 1), 128), F32),
+        ((9, 128), F32),
         ((24, 128), F32),
         ((128, 128), BF16),
         ((128, 128), BF16),
@@ -521,8 +525,12 @@
 
     field, fields, line = ((9, 128), F32), ((2, 9, 128), F32), ((1, 128), F32)
     pair, back = [((2, inner), F32), ((2, 128), F32)], ((inner // 128 * 3, 128), F32)
-    pay, outer, outer_chosen, outer_chosen_t, outer_sum, placed, inverse, *ones, partner = start(
-        obs_point, obs_count, point_jac, residuals, pt_damp, cam_jac, obs_camera, partner_mask
+    (
+        pay, cam_damp, outer, outer_chosen, outer_chosen_t, outer_sum, placed, inverse,
+        *ones, partner,
+    ) = start(
+        obs_point, obs_count, point_jac, residuals, pt_damp, cam_jac, obs_camera, cam_damp,
+        partner_mask,
     )
     pay = rows_over_dev(pay)
     sums, chosen, chosen_t = call(

time: 153 us -> 153 us (level)
  no operation moved by 1% of the time
where the time goes in v6:
time: 153 us; the launch traced here: 152 us
  blocking collectives  144 us (94%)
  Pallas kernels  7.23 us (5%)
    all_to_all x3, blocking collectives, rows_over_dev(): got = lax.all_to_all(blocks, 'dev', split_axis=0, concat_axis=0, tiled=True)  75.1 us
    all_to_all x3, blocking collectives, over_group(): lax.all_to_all(values, 'group', split_axis=0, concat_axis=0, tiled=True)  34.6 us
    all_to_all x2, blocking collectives, over_dev(): lax.all_to_all(values, 'dev', split_axis=1, concat_axis=1, tiled=True)  34.1 us
    pallas_call x8, Pallas kernels, call(): pl.pallas_call(kernel, name=name, out_shape=[jax.ShapeDtypeStruct(*shape)...  4.66 us

profile of v6, /device:TPU:1, one launch (start us, length us, event | category | flops | bytes accessed | tf_op | source)
XLA Modules:
  0.0 152.4 jit_solution(11342293340645029882)
XLA Ops:
  1.3 2.6 %setup.1 = (f32[672,128]{1,0:T(8,128)S(1)}, f32[9,128]{1,0:T(8,128)S(1)}, f32[24,128]{1,0:T(8,128)S(1)}, bf16[128,128]{1,0:T(8,128)(2,1)S(1)}, bf16[128,128]{1,0...) custom-call(s32[4224]{0:T(1024)} %refs_0_.1, ...), custom_call_target="tpu_custom_call" | custom-call | tf_op jit(solution)/shard_map/setup/pallas_call | solution.py:493
  3.9 42.4 %all_to_all.52 = f32[32,21,1,128]{3,2,1,0:T(1,128)S(1)} all-to-all(f32[32,21,1,128]{3,2,1,0:T(1,128)S(1)} %bitcast.15), channel_id=1, replica_groups=mesh['group'=16,'dev'=32] {'dev'}, dimensions={0} | all-to-all | bytes 688128 | tf_op jit(solution)/shard_map/all_to_all | solution.py:517
  46.3 0.7 start_sum.1
  47.0 15.2 %all_to_all.53.group_ref = f32[16,36,128]{2,1,0:T(8,128)S(1)} all-to-all(f32[16,36,128]{2,1,0:T(8,128)S(1)} %get-tuple-element.37.sent_ref), channel_id=1, replica_groups=mesh['group'=16,'dev'=32] {'group'}, dimensions={0} | all-to-all | bytes 589824 | tf_op jit(solution)/shard_map/all_to_all | solution.py:521
  62.2 0.3 start.1
  62.5 16.6 %all_to_all.54 = f32[2,32,128]{2,0,1:T(2,128)S(1)} all-to-all(f32[2,32,128]{2,0,1:T(2,128)S(1)} %bitcast.23), channel_id=1, replica_groups=mesh['group'=16,'dev'=32] {'dev'}, dimensions={1} | all-to-all | bytes 65536 | tf_op jit(solution)/shard_map/all_to_all | solution.py:513
  79.1 0.8 point_first.1
  79.9 16.3 %all_to_all.55 = f32[32,3,1,128]{3,2,1,0:T(1,128)S(1)} all-to-all(f32[32,3,1,128]{3,2,1,0:T(1,128)S(1)} %bitcast.21), channel_id=1, replica_groups=mesh['group'=16,'dev'=32] {'dev'}, dimensions={0} | all-to-all | bytes 98304 | tf_op jit(solution)/shard_map/all_to_all | solution.py:517
  96.3 0.3 image.1.sent_ref
  96.6 9.9 %all_to_all.56.group_ref = f32[16,19,128]{2,1,0:T(8,128)S(1)} all-to-all(f32[16,19,128]{2,1,0:T(8,128)S(1)} %image.1.sent_ref), channel_id=1, replica_groups=mesh['group'=16,'dev'=32] {'group'}, dimensions={0} | all-to-all | bytes 311296 | tf_op jit(solution)/shard_map/all_to_all | solution.py:521
  106.5 0.4 camera.1
  106.9 17.5 %all_to_all.57 = f32[2,32,128]{2,0,1:T(2,128)S(1)} all-to-all(f32[2,32,128]{2,0,1:T(2,128)S(1)} %bitcast.22), channel_id=1, replica_groups=mesh['group'=16,'dev'=32] {'dev'}, dimensions={1} | all-to-all | bytes 65536 | tf_op jit(solution)/shard_map/all_to_all | solution.py:513
  124.4 0.8 point_next.1
  125.2 16.3 %all_to_all.58 = f32[32,3,1,128]{3,2,1,0:T(1,128)S(1)} all-to-all(f32[32,3,1,128]{3,2,1,0:T(1,128)S(1)} %bitcast.20), channel_id=1, replica_groups=mesh['group'=16,'dev'=32] {'dev'}, dimensions={0} | all-to-all | bytes 98304 | tf_op jit(solution)/shard_map/all_to_all | solution.py:517
  141.6 0.3 pair.1
  141.9 9.5 %all_to_all.59.group_ref = f32[16,10,128]{2,1,0:T(8,128)S(1)} all-to-all(f32[16,10,128]{2,1,0:T(8,128)S(1)} %get-tuple-element.61), channel_id=1, replica_groups=mesh['group'=16,'dev'=32] {'group'}, dimensions={0} | all-to-all | bytes 163840 | tf_op jit(solution)/shard_map/all_to_all | solution.py:521
  151.4 1.0 last.1

commit v7 on v6

--- a/solution.py
+++ b/solution.py
@@ -261,10 +261,8 @@
         chosen_t_ref[lo:hi, :] = chosen_t
         sums = added(sums, start_terms(owned, chosen_t))
     sums = both_halves(sums)
-    for i in range(group_ref.shape[0]):
-        group_ref[i, 0:9, :] = sums[0:9]
-        group_ref[i, 9:18, :] = sums[9:18] + damp_ref[...]
-        group_ref[i, 18:36, :] = outer_sum_ref[...]
+    block = jnp.concatenate([sums[0:9], sums[9:18] + damp_ref[...], outer_sum_ref[...]], 0)
+    put_blocks(group_ref, block)
 
 
 def twice(values):
@@ -288,11 +286,17 @@
     put_rows(out_ref, apply_cams(outer_ref[...], twice(twin), outer_chosen_ref[...]))
 
 
-def partner_block(partner_ref, group_ref, lo, hi):
+def put_blocks(group_ref, block):
+    rows = block.shape[0]
+    for at in range(0, group_ref.shape[0], rows):
+        group_ref[at : at + rows, :] = block
+
+
+def partner_block(partner_ref, group_ref, rows, count):
     partner = partner_ref[...]
-    out = group_ref[0, lo:hi, :]
-    for i in range(1, group_ref.shape[0]):
-        out = jnp.where(partner == i, group_ref[i, lo:hi, :], out)
+    out = group_ref[0:count, :]
+    for i in range(1, group_ref.shape[0] // rows):
+        out = jnp.where(partner == i, group_ref[rows * i : rows * i + count, :], out)
     return out
 
 
@@ -301,8 +305,8 @@
     outer_chosen_ref,
     in_ref, out_ref, rem_ref, pre_ref, dir_ref,
 ):
-    theirs = partner_block(partner_ref, group_ref, 0, 36)
-    sums = [sent_ref[0, 0:18, :] + theirs[18:36], theirs[0:18] + outer_sum_ref[...]]
+    theirs = partner_block(partner_ref, group_ref, 36, 36)
+    sums = [sent_ref[0:18, :] + theirs[18:36], theirs[0:18] + outer_sum_ref[...]]
     for i in range(2):
         remainder = -sums[i][0:9]
         precond = 1.0 / sums[i][9:18]
@@ -397,16 +401,13 @@
 
 def image_kernel(back_ref, outer_sum_ref, pay_ref, chosen_t_ref, damp_ref, dir_ref, group_ref):
     image, partial = inner_image(back_ref, pay_ref, chosen_t_ref, damp_ref, dir_ref[0])
-    for i in range(group_ref.shape[0]):
-        group_ref[i, 0:9, :] = image
-        group_ref[i, 9:18, :] = outer_sum_ref[...]
-        group_ref[i, 18:19, :] = partial
+    put_blocks(group_ref, jnp.concatenate([image, outer_sum_ref[...], partial], 0))
 
 
 def group_total(group_ref, r):
-    row = group_ref[0, r : r + 1, :]
-    for i in range(1, group_ref.shape[0]):
-        row = row + group_ref[i, r : r + 1, :]
+    row = group_ref[r : r + 1, :]
+    for at in range(r + 1 + r, group_ref.shape[0], r + 1):
+        row = row + group_ref[at : at + 1, :]
     return row
 
 
@@ -419,8 +420,8 @@
     sums_ref[...] = sums
     norm, bend = scalars(sums, 2)
     step = norm / bend
-    theirs = partner_block(partner_ref, group_ref, 0, 18)
-    images = [sent_ref[0, 0:9, :] + theirs[9:18], theirs[0:9] + outer_sum_ref[...]]
+    theirs = partner_block(partner_ref, group_ref, 19, 18)
+    images = [sent_ref[0:9, :] + theirs[9:18], theirs[0:9] + outer_sum_ref[...]]
     image_ref[...] = images[0]
     for i in range(2):
         remainder = rem_ref[i] - step * images[i]
@@ -437,9 +438,7 @@
 ):
     image, partial = inner_image(back_ref, pay_ref, chosen_t_ref, damp_ref, scaled_ref[0])
     image_ref[...] = image
-    for i in range(group_ref.shape[0]):
-        group_ref[i, 0:9, :] = outer_sum_ref[...]
-        group_ref[i, 9:10, :] = partial
+    put_blocks(group_ref, jnp.concatenate([outer_sum_ref[...], partial], 0))
 
 
 def last_kernel(
@@ -451,7 +450,7 @@
     ratio = next_norm / norm
     next_bend = next_bend + ratio * (2.0 * cross + ratio * bend)
     step = next_norm / next_bend
-    theirs = partner_block(partner_ref, group_ref, 0, 9)
+    theirs = partner_block(partner_ref, group_ref, 10, 9)
     image = inner_ref[...] + theirs + ratio * image_ref[...]
     direction = dir_ref[0]
     update_ref[...] = norm / bend * direction + step * (scaled_ref[0] + ratio * direction)
@@ -518,10 +517,12 @@
         return got.reshape(values.shape)
 
     def over_group(values):
-        return lax.all_to_all(values, "group", split_axis=0, concat_axis=0, tiled=True)
+        blocks = values.reshape(groups, -1, 1, 128)
+        got = lax.all_to_all(blocks, "group", split_axis=0, concat_axis=0, tiled=True)
+        return got.reshape(values.shape)
 
     def sends(rows):
-        return ((groups, rows, 128), F32)
+        return ((groups * rows, 128), F32)
 
     field, fields, line = ((9, 128), F32), ((2, 9, 128), F32), ((1, 128), F32)
     pair, back = [((2, inner), F32), ((2, 128), F32)], ((inner // 128 * 3, 128), F32)

time: 153 us -> 152 us (level)
  no operation moved by 1% of the time
where the time goes in v7:
time: 152 us
  blocking collectives  143 us (94%)
  Pallas kernels  7.23 us (5%)
    all_to_all x3, blocking collectives, rows_over_dev(): got = lax.all_to_all(blocks, 'dev', split_axis=0, concat_axis=0, tiled=True)  75.1 us
    all_to_all x2, blocking collectives, over_dev(): lax.all_to_all(values, 'dev', split_axis=1, concat_axis=1, tiled=True)  34.2 us
    all_to_all x3, blocking collectives, over_group(): lax.all_to_all(blocks, 'group', split_axis=0, concat_axis=0, tiled=True)  33.7 us
    pallas_call x8, Pallas kernels, call(): pl.pallas_call(kernel, name=name, out_shape=[jax.ShapeDtypeStruct(*shape)...  4.66 us

profile of v7, /device:TPU:1, one launch (start us, length us, event | category | flops | bytes accessed | tf_op | source)
XLA Modules:
  0.0 151.6 jit_solution(9470222875704636790)
XLA Ops:
  1.3 2.6 %setup.1 = (f32[672,128]{1,0:T(8,128)S(1)}, f32[9,128]{1,0:T(8,128)S(1)}, f32[24,128]{1,0:T(8,128)S(1)}, bf16[128,128]{1,0:T(8,128)(2,1)S(1)}, bf16[128,128]{1,0...) custom-call(s32[4224]{0:T(1024)} %refs_0_.1, ...), custom_call_target="tpu_custom_call" | custom-call | tf_op jit(solution)/shard_map/setup/pallas_call | solution.py:492
  3.9 42.4 %all_to_all.52 = f32[32,21,1,128]{3,2,1,0:T(1,128)S(1)} all-to-all(f32[32,21,1,128]{3,2,1,0:T(1,128)S(1)} %bitcast.25), channel_id=1, replica_groups=mesh['group'=16,'dev'=32] {'dev'}, dimensions={0} | all-to-all | bytes 688128 | tf_op jit(solution)/shard_map/all_to_all | solution.py:516
  46.3 0.7 start_sum.1
  47.0 14.8 %all_to_all.53 = f32[16,36,1,128]{3,2,1,0:T(1,128)S(1)} all-to-all(f32[16,36,1,128]{3,2,1,0:T(1,128)S(1)} %bitcast.22), channel_id=1, replica_groups=mesh['group'=16,'dev'=32] {'group'}, dimensions={0} | all-to-all | bytes 589824 | tf_op jit(solution)/shard_map/all_to_all | solution.py:521
  61.8 0.3 start.1
  62.2 16.6 %all_to_all.54 = f32[2,32,128]{2,0,1:T(2,128)S(1)} all-to-all(f32[2,32,128]{2,0,1:T(2,128)S(1)} %bitcast.35), channel_id=1, replica_groups=mesh['group'=16,'dev'=32] {'dev'}, dimensions={1} | all-to-all | bytes 65536 | tf_op jit(solution)/shard_map/all_to_all | solution.py:512
  78.8 0.8 point_first.1
  79.6 16.3 %all_to_all.55 = f32[32,3,1,128]{3,2,1,0:T(1,128)S(1)} all-to-all(f32[32,3,1,128]{3,2,1,0:T(1,128)S(1)} %bitcast.33), channel_id=1, replica_groups=mesh['group'=16,'dev'=32] {'dev'}, dimensions={0} | all-to-all | bytes 98304 | tf_op jit(solution)/shard_map/all_to_all | solution.py:516
  95.9 0.3 image.1.sent_ref
  96.2 9.6 %all_to_all.56 = f32[16,19,1,128]{3,2,1,0:T(1,128)S(1)} all-to-all(f32[16,19,1,128]{3,2,1,0:T(1,128)S(1)} %bitcast.21), channel_id=1, replica_groups=mesh['group'=16,'dev'=32] {'group'}, dimensions={0} | all-to-all | bytes 311296 | tf_op jit(solution)/shard_map/all_to_all | solution.py:521
  105.8 0.4 camera.1
  106.2 17.6 %all_to_all.57 = f32[2,32,128]{2,0,1:T(2,128)S(1)} all-to-all(f32[2,32,128]{2,0,1:T(2,128)S(1)} %bitcast.34), channel_id=1, replica_groups=mesh['group'=16,'dev'=32] {'dev'}, dimensions={1} | all-to-all | bytes 65536 | tf_op jit(solution)/shard_map/all_to_all | solution.py:512
  123.8 0.8 point_next.1
  124.6 16.3 %all_to_all.58 = f32[32,3,1,128]{3,2,1,0:T(1,128)S(1)} all-to-all(f32[32,3,1,128]{3,2,1,0:T(1,128)S(1)} %bitcast.32), channel_id=1, replica_groups=mesh['group'=16,'dev'=32] {'dev'}, dimensions={0} | all-to-all | bytes 98304 | tf_op jit(solution)/shard_map/all_to_all | solution.py:516
  141.0 0.3 pair.1
  141.3 9.3 %all_to_all.59 = f32[16,10,1,128]{3,2,1,0:T(1,128)S(1)} all-to-all(f32[16,10,1,128]{3,2,1,0:T(1,128)S(1)} %bitcast.31), channel_id=1, replica_groups=mesh['group'=16,'dev'=32] {'group'}, dimensions={0} | all-to-all | bytes 163840 | tf_op jit(solution)/shard_map/all_to_all | solution.py:521
  150.6 1.0 last.1
